TPU v7x, 1024 devices: a whole 4x8x16 slice. The times are simulated.
1024 devices in a mesh: fsdp: 16 (over y, core), grp: 64 (over x, z).
Axes of the slice: x: 4, y: 8, z: 16, core: 2. Of those that a mesh axis runs over, the one named last changes fastest.
Arguments:
- grad: bfloat16 [64, 512, 8192], P('grp', 'fsdp'), may hold values from -30 to 30
- table: int32 [64, 16], P('grp'), may hold values from 0 to 15, each once within a row
- left_stat: bfloat16 [64, 16, 512, 512], P('grp', 'fsdp'), may hold values from -4 to 4, as said below
- right_stat: bfloat16 [64, 16, 512, 512], P('grp', 'fsdp'), may hold values from -4 to 4, as said below
- left_basis: bfloat16 [64, 16, 512, 512], P('grp', 'fsdp'), may hold values from -4 to 4, as said below
- right_basis: bfloat16 [64, 16, 512, 512], P('grp', 'fsdp'), may hold values from -4 to 4, as said below
- row_moment: float32 [64, 16, 512], P('grp', 'fsdp'), may hold values from 0.05 to 1
- col_moment: float32 [64, 16, 512], P('grp', 'fsdp'), may hold values from 0.05 to 1
Outputs:
- update: bfloat16 [64, 512, 8192], P('grp', 'fsdp')
- row_next: float32 [64, 16, 512], P('grp', 'fsdp')
- col_next: float32 [64, 16, 512], P('grp', 'fsdp')
Inputs may be any that keep to these rules, and one draw needn't show every extreme that they name: Each row of table lists every owner 0 to 15 once. `left_stat`: symmetric with a dominant diagonal. `right_stat`: symmetric with a dominant diagonal. `left_basis`: nonsingular. `right_basis`: nonsingular.
All inputs are finite; a program needn't handle non-finite values.
Results may differ from a plain program's by a relative error of at most 0.01.
Values may be sent and summed in bfloat16 or wider, within the bound.
No kernel may reach another device: no remote copies, remote signals or barrier semaphores. Data moves between devices by JAX's collectives and lax.ppermute only.
A program may use at most 32 MiB of HBM per device.

v0:
```python
import jax
import jax.numpy as jnp
from jax import lax
from jax.sharding import PartitionSpec as P

DECAY_STAT = 0.95
DECAY_MOMENT = 0.95
CLIP_RMS = 0.5
EPSILON = 1e-08


def from_everyone(shard, axis):
    size = lax.axis_size(axis)
    return lax.all_to_all(
        jnp.broadcast_to(shard[None], (size, *shard.shape)), axis, 0, 0, tiled=True
    )


def of_everyone(shard, axis):
    everything = from_everyone(shard, axis)
    return jnp.sum(everything, axis=0)


def refresh(stat, gram, basis, clip):
    new_stat = DECAY_STAT * stat.astype(jnp.float32) + (1.0 - DECAY_STAT) * clip * clip * gram
    product = jnp.dot(new_stat, basis.astype(jnp.float32), precision=lax.Precision.HIGHEST)
    inner = jnp.dot(product.T, product, precision=lax.Precision.HIGHEST)
    factor = jnp.linalg.cholesky(inner)
    ortho = jax.scipy.linalg.solve_triangular(factor, product.T, lower=True).T
    return ortho.astype(jnp.bfloat16)


def soap_block(block, clip, left_stat, right_stat, left_basis, right_basis, row_moment, col_moment):
    left_gram = jnp.dot(block, block.T, preferred_element_type=jnp.float32)
    right_gram = jnp.dot(block.T, block, preferred_element_type=jnp.float32)
    left_new = refresh(left_stat, left_gram, left_basis, clip)
    right_new = refresh(right_stat, right_gram, right_basis, clip)
    half = jnp.dot(left_new.T, block, preferred_element_type=jnp.float32).astype(jnp.bfloat16)
    rotated = clip * jnp.dot(half, right_new, preferred_element_type=jnp.float32)
    square = rotated * rotated
    row_next = DECAY_MOMENT * row_moment + (1.0 - DECAY_MOMENT) * jnp.mean(square, axis=1)
    col_next = DECAY_MOMENT * col_moment + (1.0 - DECAY_MOMENT) * jnp.mean(square, axis=0)
    second = row_next[:, None] * col_next[None, :] / jnp.mean(row_next)
    normed = (rotated / (jnp.sqrt(second) + EPSILON)).astype(jnp.bfloat16)
    back = jnp.dot(left_new, normed, preferred_element_type=jnp.float32).astype(jnp.bfloat16)
    update = jnp.dot(back, right_new.T, preferred_element_type=jnp.float32).astype(jnp.bfloat16)
    return (update, row_next, col_next)


def shards(grad, table, left_stat, right_stat, left_basis, right_basis, row_moment, col_moment):
    order_size = left_stat.shape[-1]
    owners = lax.axis_size("fsdp")
    my_rows = grad.shape[1]
    inverse = jnp.argsort(table[0])
    stripes = grad[0].reshape(my_rows, owners, order_size)
    outgoing = jnp.take(stripes, inverse, axis=1)
    block = lax.all_to_all(outgoing, "fsdp", split_axis=1, concat_axis=0, tiled=True).reshape(
        order_size, order_size
    )
    local = jnp.sum(jnp.square(grad.astype(jnp.float32)))
    partial_sum = of_everyone(local, "fsdp")
    total = of_everyone(partial_sum, "grp")
    count = float(lax.axis_size("grp") * owners * order_size * order_size)
    clip = CLIP_RMS / jnp.sqrt(total / count + 1e-06)
    update, row_next, col_next = soap_block(
        block,
        clip,
        left_stat[0, 0],
        right_stat[0, 0],
        left_basis[0, 0],
        right_basis[0, 0],
        row_moment[0, 0],
        col_moment[0, 0],
    )
    pieces = update.reshape(owners, my_rows, order_size)
    returned = lax.all_to_all(pieces, "fsdp", split_axis=0, concat_axis=2, tiled=True)
    placed = jnp.take(returned.reshape(my_rows, owners, order_size), table[0], axis=1)
    result = placed.reshape(1, my_rows, owners * order_size)
    return (result, row_next[None, None, :], col_next[None, None, :])


def solution(mesh):
    in_specs = (
        P("grp", "fsdp", None),
        P("grp", None),
        P("grp", "fsdp", None, None),
        P("grp", "fsdp", None, None),
        P("grp", "fsdp", None, None),
        P("grp", "fsdp", None, None),
        P("grp", "fsdp", None),
        P("grp", "fsdp", None),
    )
    out_specs = (P("grp", "fsdp", None), P("grp", "fsdp", None), P("grp", "fsdp", None))
    return jax.shard_map(shards, mesh=mesh, in_specs=in_specs, out_specs=out_specs, check_vma=False)
```

profile of v0, /device:TPU:1, one launch (start us, length us, event | category | flops | bytes accessed | tf_op | source)
XLA Modules:
  0.0 427.5 jit_solution(11650046955527485578)
XLA Ops:
  3.9 17.4 %all-to-all-start = ((f32[16,1,1]{2,1,0:T(1,128)}), f32[16,1,1]{2,1,0:T(1,128)S(1)}, u32[]{:S(2)}, u32[]{:S(2)}) async-start(f32[16,1,1]{2,1,0:T(1,128)} %broadcast_in_dim.13), calls=%async_computation | async-start | bytes 16384 | tf_op jit(solution)/shard_map/all_to_all | solution.py:14
  24.3 4.0 all-to-all-done
  30.2 13.1 %all-to-all-start.1 = ((f32[64,1,1]{2,1,0:T(1,128)}), f32[64,1,1]{2,1,0:T(1,128)S(1)}, u32[]{:S(2)}, u32[]{:S(2)}) async-start(f32[64,1,1]{2,1,0:T(1,128)} %broadcast_in_dim.14), calls=%async_computation.1 | async-start | bytes 65536 | tf_op jit(solution)/shard_map/all_to_all | solution.py:14
  44.2 12.4 %all-to-all-done.1 = f32[64,1,1]{2,1,0:T(1,128)S(1)} async-done(((f32[64,1,1]{2,1,0:T(1,128)}), f32[64,1,1]{2,1,0:T(1,128)S(1)}, u32[]{:S(2)}, u32[]{:S(2)}) %all-to-all-start.1) | async-done | bytes 288 | tf_op jit(solution)/shard_map/all_to_all | solution.py:14
  56.6 5.8 %all-to-all-start.2 = ((bf16[32,16,512]{2,0,1:T(8,128)(2,1)}), bf16[32,16,512]{2,0,1:T(8,128)(2,1)S(1)}, u32[]{:S(2)}, u32[]{:S(2)}) async-start(bf16[32,16,512]{2,0,1:T(8,128)(2,1)} %select_bitcast_fusion.1), calls=%async_computation.2 | async-start | bytes 1048576 | tf_op jit(solution)/shard_map/all_to_all | solution.py:57
  63.8 15.5 %all-to-all-done.2 = bf16[32,16,512]{2,0,1:T(8,128)(2,1)S(1)} async-done(((bf16[32,16,512]{2,0,1:T(8,128)(2,1)}), bf16[32,16,512]{2,0,1:T(8,128)(2,1)S(1)}, u32[]{:S(2)}, u32[]{:S(2)}) %all-to-all-start.2) | async-done | bytes 524320 | tf_op jit(solution)/shard_map/all_to_all | solution.py:57
  86.3 11.7 %cholesky.286 = f32[128,128]{1,0:T(8,128)S(1)} custom-call(f32[128,128]{1,0:T(8,128)S(1)} %cholesky.426), custom_call_target="Cholesky" | custom-call | tf_op jit(solution)/shard_map/jit(cholesky)/cholesky | solution.py:28
  98.1 9.8 %custom-call.27 = f32[1,128,128]{1,2,0:T(8,128)S(1)} custom-call(f32[1,128,128]{2,1,0:T(8,128)S(1)} %get-tuple-element.57), custom_call_target="InvertDiagBlocksLowerTriangular" | custom-call | tf_op jit(solution)/shard_map/jit(cholesky)/cholesky | solution.py:28
  110.6 11.9 %cholesky.305 = f32[128,128]{1,0:T(8,128)S(1)} custom-call(f32[128,128]{1,0:T(8,128)S(1)} %cholesky.430), custom_call_target="Cholesky" | custom-call | tf_op jit(solution)/shard_map/jit(cholesky)/cholesky | solution.py:28
  122.5 9.8 %custom-call.28 = f32[1,128,128]{1,2,0:T(8,128)S(1)} custom-call(f32[1,128,128]{2,1,0:T(8,128)S(1)} %get-tuple-element.54), custom_call_target="InvertDiagBlocksLowerTriangular" | custom-call | tf_op jit(solution)/shard_map/jit(cholesky)/cholesky | solution.py:28
  133.9 11.7 %cholesky.326 = f32[128,128]{1,0:T(8,128)S(1)} custom-call(f32[128,128]{1,0:T(8,128)S(1)} %cholesky.435), custom_call_target="Cholesky" | custom-call | tf_op jit(solution)/shard_map/jit(cholesky)/cholesky | solution.py:28
  146.3 9.8 %custom-call.29 = f32[1,128,128]{1,2,0:T(8,128)S(1)} custom-call(f32[1,128,128]{2,1,0:T(8,128)S(1)} %get-tuple-element.51), custom_call_target="InvertDiagBlocksLowerTriangular" | custom-call | tf_op jit(solution)/shard_map/jit(cholesky)/cholesky | solution.py:28
  157.5 12.1 %cholesky.343 = f32[128,128]{1,0:T(8,128)S(1)} custom-call(f32[128,128]{1,0:T(8,128)S(1)} %convolution_subtract_fusion.11), custom_call_target="Cholesky" | custom-call | tf_op jit(solution)/shard_map/jit(cholesky)/cholesky | solution.py:28
  174.7 11.6 %while.4 = (s32[]{:T(128)}, f32[512,512]{1,0:T(8,128)}, s32[4,2]{0,1:T(2,128)S(1)}, f32[4,128,128]{2,1,0:T(8,128)S(1)}, s32[]{:T(128)}) while((s32[]{:T(128)}, f32[512,512]{1,0:T(8,128)}, s32[4,2]{0,1:T(2,128)S(1)}, f32[4,128,128]{2,1,0:T(8,128)S(1)}, s32[]{:T(128)}) %tuple.65), condition=%wide.while_cond, body=%wide.while_body.sunk | while | flops 2 | bytes 131181 | solution.py:29
  175.3 2.3 bitcast_dynamic-update-slice_fusion.4
  178.2 2.3 bitcast_dynamic-update-slice_fusion.4
  181.1 2.3 bitcast_dynamic-update-slice_fusion.4
  186.3 39.3 %custom-call.30 = f32[4,128,128]{1,2,0:T(8,128)S(1)} custom-call(f32[4,128,128]{2,1,0:T(8,128)S(1)} %get-tuple-element.22), custom_call_target="InvertDiagBlocksLowerTriangular" | custom-call | tf_op jit(solution)/shard_map/jit(_solve_triangular)/triangular_solve | solution.py:29
  230.4 2.5 convolution_subtract_fusion.5
  241.6 11.7 %cholesky.358 = f32[128,128]{1,0:T(8,128)S(1)} custom-call(f32[128,128]{1,0:T(8,128)S(1)} %cholesky.439), custom_call_target="Cholesky" | custom-call | tf_op jit(solution)/shard_map/jit(cholesky)/cholesky | solution.py:28
  253.4 9.9 %custom-call.31 = f32[1,128,128]{1,2,0:T(8,128)S(1)} custom-call(f32[1,128,128]{2,1,0:T(8,128)S(1)} %get-tuple-element.67), custom_call_target="InvertDiagBlocksLowerTriangular" | custom-call | tf_op jit(solution)/shard_map/jit(cholesky)/cholesky | solution.py:28
  266.6 11.7 %cholesky.377 = f32[128,128]{1,0:T(8,128)S(1)} custom-call(f32[128,128]{1,0:T(8,128)S(1)} %cholesky.443), custom_call_target="Cholesky" | custom-call | tf_op jit(solution)/shard_map/jit(cholesky)/cholesky | solution.py:28
  278.4 9.8 %custom-call.32 = f32[1,128,128]{1,2,0:T(8,128)S(1)} custom-call(f32[1,128,128]{2,1,0:T(8,128)S(1)} %get-tuple-element.64), custom_call_target="InvertDiagBlocksLowerTriangular" | custom-call | tf_op jit(solution)/shard_map/jit(cholesky)/cholesky | solution.py:28
  291.3 13.3 %cholesky.398 = f32[128,128]{1,0:T(8,128)} custom-call(f32[128,128]{1,0:T(8,128)} %cholesky.448), custom_call_target="Cholesky" | custom-call | tf_op jit(solution)/shard_map/jit(cholesky)/cholesky | solution.py:28
  306.8 11.3 %custom-call.33 = f32[1,128,128]{1,2,0:T(8,128)} custom-call(f32[1,128,128]{2,1,0:T(8,128)} %get-tuple-element.61), custom_call_target="InvertDiagBlocksLowerTriangular" | custom-call | tf_op jit(solution)/shard_map/jit(cholesky)/cholesky | solution.py:28
  320.3 11.7 %cholesky.415 = f32[128,128]{1,0:T(8,128)S(1)} custom-call(f32[128,128]{1,0:T(8,128)S(1)} %convolution_subtract_fusion.10), custom_call_target="Cholesky" | custom-call | tf_op jit(solution)/shard_map/jit(cholesky)/cholesky | solution.py:28
  337.1 11.6 %while.5 = (s32[]{:T(128)}, f32[512,512]{1,0:T(8,128)}, s32[4,2]{0,1:T(2,128)S(1)}, f32[4,128,128]{2,1,0:T(8,128)S(1)}, s32[]{:T(128)}) while((s32[]{:T(128)}, f32[512,512]{1,0:T(8,128)}, s32[4,2]{0,1:T(2,128)S(1)}, f32[4,128,128]{2,1,0:T(8,128)S(1)}, s32[]{:T(128)}) %tuple.68), condition=%wide.while_cond.clone, body=%wide.while_body.clone.sunk | while | flops 2 | bytes 131181 | solution.py:29
  348.6 39.6 %custom-call.34 = f32[4,128,128]{1,2,0:T(8,128)S(1)} custom-call(f32[4,128,128]{2,1,0:T(8,128)S(1)} %get-tuple-element.23), custom_call_target="InvertDiagBlocksLowerTriangular" | custom-call | tf_op jit(solution)/shard_map/jit(_solve_triangular)/triangular_solve | solution.py:29
  392.9 2.4 convolution_subtract_fusion.4
  401.8 3.1 convolution_convert_fusion
  405.0 3.5 all-to-all-start.3
  408.5 16.7 %all-to-all-done.3 = bf16[16,32,512]{2,1,0:T(8,128)(2,1)S(1)} async-done(((bf16[16,32,512]{2,1,0:T(8,128)(2,1)}), bf16[16,32,512]{2,1,0:T(8,128)(2,1)S(1)}, u32[]{:S(2)}, u32[]{:S(2)}) %all-to-all-start.3) | async-done | bytes 524320 | tf_op jit(solution)/shard_map/all_to_all | solution.py:76
  (147 shorter events, 81.0 us)
Async XLA Ops:
  0.6 79.1 %copy-start = (bf16[1,1,512,512]{3,2,1,0:T(8,128)(2,1)S(1)}, bf16[1,1,512,512]{3,2,1,0:T(8,128)(2,1)}, u32[]{:S(2)}) copy-start(bf16[1,1,512,512]{3,2,1,0:T(8,128)(2,1)} %param.17) | copy-start | bytes 1572868
  0.6 22.6 %copy-start.5 = (bf16[1,32,8192]{2,1,0:T(8,128)(2,1)S(1)}, bf16[1,32,8192]{2,1,0:T(8,128)(2,1)}, u32[]{:S(2)}) copy-start(bf16[1,32,8192]{2,1,0:T(8,128)(2,1)} %param.13) | copy-start | bytes 1572868
  3.9 24.4 %all-to-all-start = ((f32[16,1,1]{2,1,0:T(1,128)}), f32[16,1,1]{2,1,0:T(1,128)S(1)}, u32[]{:S(2)}, u32[]{:S(2)}) async-start(f32[16,1,1]{2,1,0:T(1,128)} %broadcast_in_dim.13), calls=%async_computation | async-start | bytes 16384 | tf_op jit(solution)/shard_map/all_to_all | solution.py:14
  21.3 0.7 copy-start.17
  30.2 26.4 %all-to-all-start.1 = ((f32[64,1,1]{2,1,0:T(1,128)}), f32[64,1,1]{2,1,0:T(1,128)S(1)}, u32[]{:S(2)}, u32[]{:S(2)}) async-start(f32[64,1,1]{2,1,0:T(1,128)} %broadcast_in_dim.14), calls=%async_computation.1 | async-start | bytes 65536 | tf_op jit(solution)/shard_map/all_to_all | solution.py:14
  44.2 35.0 %copy-start.10 = (bf16[1,1,512,512]{3,2,1,0:T(8,128)(2,1)S(1)}, bf16[1,1,512,512]{3,2,1,0:T(8,128)(2,1)}, u32[]{:S(2)}) copy-start(bf16[1,1,512,512]{3,2,1,0:T(8,128)(2,1)} %param.15) | copy-start | bytes 1572868
  56.6 22.6 %all-to-all-start.2 = ((bf16[32,16,512]{2,0,1:T(8,128)(2,1)}), bf16[32,16,512]{2,0,1:T(8,128)(2,1)S(1)}, u32[]{:S(2)}, u32[]{:S(2)}) async-start(bf16[32,16,512]{2,0,1:T(8,128)(2,1)} %select_bitcast_fusion.1), calls=%async_computation.2 | async-start | bytes 1048576 | tf_op jit(solution)/shard_map/all_to_all | solution.py:57
  85.3 1.0 copy-start.1
  227.9 2.4 copy-start.3
  230.3 2.5 copy-start.6
  230.3 3.6 copy-start.16
  233.9 1.0 copy-start.9
  240.6 1.0 copy-start.2
  265.9 0.7 copy-start.8
  388.2 1.9 copy-start.11
  390.5 2.0 copy-start.12
  392.9 2.9 copy-start.7
  395.4 1.0 copy-start.4
  395.4 1.0 copy-start.13
  398.1 0.7 copy-start.14
  399.3 0.7 copy-start.15
  405.0 20.2 %all-to-all-start.3 = ((bf16[16,32,512]{2,1,0:T(8,128)(2,1)}), bf16[16,32,512]{2,1,0:T(8,128)(2,1)S(1)}, u32[]{:S(2)}, u32[]{:S(2)}) async-start(bf16[16,32,512]{2,1,0:T(8,128)(2,1)} %bitcast.39), calls=%async_computation.3 | async-start | bytes 1048576 | tf_op jit(solution)/shard_map/all_to_all | solution.py:76
where the time goes:
time: 432 us; the launch traced here: 427 us
  other arithmetic  253 us (59%)
  waiting for transfers between devices  48.5 us (11%)
  starting transfers between devices  39.8 us (9%)
  matrix products  39.8 us (9%)
  local copies, waits for them, and re-layouts  37.8 us (9%)
  between operations  8.01 us (2%)
    another operation x28, other arithmetic, refresh(): factor = jnp.linalg.cholesky(inner)  162 us
    another operation x5, other arithmetic, refresh(): ortho = jax.scipy.linalg.solve_triangular(factor, product.T, lower=True).T  81.1 us
    all_to_all x2, starting transfers between devices, from_everyone(): lax.all_to_all(jnp.broadcast_to(shard[None], (size, *shard.shape)), axis,...  30.5 us
    another operation x27, local copies, waits for them, and re-layouts, refresh(): ortho = jax.scipy.linalg.solve_triangular(factor, product.T, lower=True).T  23 us
    all_to_all x1, waiting for transfers between devices, shards(): lax.all_to_all(pieces, 'fsdp', split_axis=0, concat_axis=2, tiled=True)  16.7 us
    all_to_all x2, waiting for transfers between devices, from_everyone(): lax.all_to_all(jnp.broadcast_to(shard[None], (size, *shard.shape)), axis,...  16.4 us
    another operation x14, matrix products, refresh(): ortho = jax.scipy.linalg.solve_triangular(factor, product.T, lower=True).T  15.7 us
    all_to_all x1, waiting for transfers between devices, shards(): lax.all_to_all(outgoing, 'fsdp', split_axis=1, concat_axis=0, tiled=True)  15.5 us
  transfers between devices with their start and end apart: 4, of which 4 were waited for; matrix products, arithmetic and copies ran while one was open for 1% of the time, Pallas kernels for 0%

commit v1 on v0

v1 whole, which is shorter than its diff:
```python
import jax
import jax.numpy as jnp
from jax import lax
from jax.experimental import pallas as pl
from jax.experimental.pallas import tpu as pltpu
from jax.sharding import PartitionSpec as P

DECAY_STAT = 0.95
DECAY_MOMENT = 0.95
CLIP_RMS = 0.5
EPSILON = 1e-08
F32 = jnp.float32
BF16 = jnp.bfloat16
TILE = 8
NB = 128
NT = NB // TILE
NN = (((1,), (0,)), ((), ()))
NT_DIMS = (((1,), (1,)), ((), ()))
TN = (((0,), (0,)), ((), ()))


def mm(a, b, dims=NN):
    return lax.dot_general(a, b, dims, preferred_element_type=F32)


def mm_full(a, b, dims=NN):
    return lax.dot_general(a, b, dims, precision=lax.Precision.HIGHEST, preferred_element_type=F32)


def split3(x):
    high = x.astype(BF16)
    rest = x - high.astype(F32)
    mid = rest.astype(BF16)
    low = (rest - mid.astype(F32)).astype(BF16)
    return high, mid, low


def mm_split(x, exact, dims=NN):
    high, mid, low = split3(x)
    return mm(high, exact, dims) + mm(mid, exact, dims) + mm(low, exact, dims)


def lane(x, c):
    return jnp.broadcast_to(x[:, c : c + 1], (TILE, NB))


def row(x, r):
    return jnp.broadcast_to(x[r : r + 1, :], (TILE, NB))


def factor_steps(get, aug, side, out):
    lanes = lax.broadcasted_iota(jnp.int32, (TILE, NB), 1)
    subs = lax.broadcasted_iota(jnp.int32, (TILE, NB), 0)

    def at(i):
        return (side, slice(TILE * i, TILE * i + TILE), slice(None))

    for i in range(NT):
        aug[at(i)] = jnp.where(lanes == subs + TILE * i, 1.0, 0.0).astype(F32)
    for k in range(NT):
        base = TILE * k
        tile = get[at(k)]
        both = aug[at(k)]
        forward = both
        cols = [lane(tile, base + j) for j in range(TILE)]
        pivots = jnp.ones((TILE, NB), F32)
        for j in range(TILE):
            pivot = row(cols[j], j)
            pivots = jnp.where(subs == j, pivot, pivots)
            mult = cols[j] * (1.0 / pivot)
            around = jnp.where(subs == j, 0.0, mult)
            below = jnp.where(subs > j, mult, 0.0)
            for q in range(j + 1, TILE):
                cols[q] = cols[q] - around * row(cols[q], j)
            both_row = row(both, j)
            tile = tile - around * row(tile, j)
            both = both - around * both_row
            forward = forward - below * both_row
            yield
        inverse = 1.0 / pivots
        out[at(k)] = forward * lax.rsqrt(pivots)
        tile = tile * inverse
        both = both * inverse
        tile_rows = [row(tile, j) for j in range(TILE)]
        both_rows = [row(both, j) for j in range(TILE)]
        for i in range(k + 1, NT):
            old = get[at(i)]
            left = [lane(old, base + j) for j in range(TILE)]
            first = [left[j] * tile_rows[j] for j in range(TILE)]
            second = [left[j] * both_rows[j] for j in range(TILE)]
            while len(first) > 1:
                first = [first[q] + first[q + 1] for q in range(0, len(first), 2)]
                second = [second[q] + second[q + 1] for q in range(0, len(second), 2)]
            get[at(i)] = old - first[0]
            aug[at(i)] = aug[at(i)] - second[0]
        yield


def interleave(steps):
    steps = list(steps)
    while steps:
        steps = [s for s in steps if next(s, steps) is not steps]


def prep_kernel(table_ref, grad_ref, out_ref, sum_ref):
    owners, my_rows, order = out_ref.shape
    total = jnp.zeros((my_rows, order), F32)
    for j in range(owners):
        part = grad_ref[:, j * order : (j + 1) * order]
        out_ref[table_ref[0, j]] = part
        wide = part.astype(F32)
        total = total + wide * wide
    sum_ref[...] = jnp.sum(total).reshape(1, 1)


def place_kernel(table_ref, back_ref, out_ref):
    owners, my_rows, order = back_ref.shape
    for j in range(owners):
        out_ref[:, j * order : (j + 1) * order] = back_ref[table_ref[0, j]]


def early_kernel(left_stat, right_stat, left_basis, right_basis, basis_t, stat_part):
    for side, (stat, basis) in enumerate(((left_stat, left_basis), (right_stat, right_basis))):
        turned = basis[...].T
        basis_t[side] = turned
        stat_part[side] = DECAY_STAT * mm(turned, stat[...])


def gram_kernel(block_ref, basis_t, gram_part):
    block = block_ref[...]
    gram_part[0] = (1.0 - DECAY_STAT) * mm_split(mm(basis_t[0], block), block, NT_DIMS)
    gram_part[1] = (1.0 - DECAY_STAT) * mm_split(mm(basis_t[1], block, NT_DIMS), block)


def main_kernel(
    clip_ref, block_ref, stat_part, gram_part, row_ref, col_ref, update_ref, row_out, col_out,
    s_ref, a_ref, t_ref, aug_ref, w_ref, q_ref,
):
    order = block_ref.shape[0]
    clip = clip_ref[0, 0]
    for side in range(2):
        a = stat_part[side] + (clip * clip) * gram_part[side]
        a_ref[side] = a
        high, mid, low = split3(a)
        for k in range(order // NB):
            part = slice(k * NB, order)
            mine = slice(k * NB, (k + 1) * NB)
            total = mm(low[mine], high[part], NT_DIMS) + mm(high[mine], low[part], NT_DIMS)
            total = total + mm(mid[mine], mid[part], NT_DIMS)
            total = total + mm(mid[mine], high[part], NT_DIMS) + mm(high[mine], mid[part], NT_DIMS)
            s_ref[side, mine, part] = total + mm(high[mine], high[part], NT_DIMS)

    for k in range(order // NB):
        mine = slice(k * NB, (k + 1) * NB)
        for side in range(2):
            t_ref[side] = s_ref[side, mine, mine]
        interleave([factor_steps(t_ref, aug_ref, side, w_ref) for side in range(2)])
        for side in range(2):
            turned = mm_full(w_ref[side], a_ref[side, mine, :])
            q_ref[side, mine, :] = turned.astype(BF16)
            if (k + 1) * NB < order:
                rest = slice((k + 1) * NB, order)
                panel = mm_full(w_ref[side], s_ref[side, mine, rest])
                panel_t = panel.T
                s_ref[side, rest, rest] = s_ref[side, rest, rest] - mm_full(panel_t, panel)
                a_ref[side, rest, :] = a_ref[side, rest, :] - mm_full(panel_t, turned)

    block = block_ref[...]
    left_t = q_ref[0]
    right_t = q_ref[1]
    half = mm(left_t, block).astype(BF16)
    rotated = clip * mm(half, right_t, NT_DIMS)
    square = rotated * rotated
    col_next = DECAY_MOMENT * col_ref[...] + (1.0 - DECAY_MOMENT) * jnp.mean(square, axis=0, keepdims=True)
    old_rows = jnp.broadcast_to(row_ref[...], (NB, order)).T
    row_mean = jnp.broadcast_to(jnp.mean(square, axis=1, keepdims=True), (order, NB))
    row_next = DECAY_MOMENT * old_rows + (1.0 - DECAY_MOMENT) * row_mean
    col_out[...] = col_next
    across = row_next.T[0:1, :]
    row_out[...] = across
    second = row_next[:, 0:1] * col_next / jnp.mean(across)
    normed = (rotated / (jnp.sqrt(second) + EPSILON)).astype(BF16)
    back = mm(left_t, normed, TN).astype(BF16)
    update_ref[...] = mm(back, right_t).astype(BF16)


VMEM = pl.BlockSpec(memory_space=pltpu.VMEM)
SMEM = pl.BlockSpec(memory_space=pltpu.SMEM)


def call(kernel, out_shapes, in_specs, out_specs, scratch=(), flops=0, moved=0):
    return pl.pallas_call(
        kernel,
        out_shape=out_shapes,
        in_specs=in_specs,
        out_specs=out_specs,
        scratch_shapes=list(scratch),
        compiler_params=pltpu.CompilerParams(vmem_limit_bytes=48 * 2**20),
        cost_estimate=pl.CostEstimate(flops=flops, bytes_accessed=moved, transcendentals=0),
    )


def shards(grad, table, left_stat, right_stat, left_basis, right_basis, row_moment, col_moment):
    order = left_stat.shape[-1]
    owners = lax.axis_size("fsdp")
    groups = lax.axis_size("grp")
    my_rows = grad.shape[1]
    shape = jax.ShapeDtypeStruct
    cube = 2 * order**3

    outgoing, local = call(
        prep_kernel,
        (shape((owners, my_rows, order), BF16), shape((1, 1), F32)),
        [SMEM, VMEM],
        (VMEM, VMEM),
        moved=4 * owners * my_rows * order,
    )(table, grad[0])
    block = lax.all_to_all(outgoing, "fsdp", split_axis=0, concat_axis=0, tiled=True).reshape(order, order)

    basis_t, stat_part = call(
        early_kernel,
        (shape((2, order, order), BF16), shape((2, order, order), F32)),
        [VMEM] * 4,
        (VMEM, VMEM),
        flops=2 * cube,
        moved=16 * order * order,
    )(left_stat[0, 0], right_stat[0, 0], left_basis[0, 0], right_basis[0, 0])

    def sum_over(value, axis, size):
        sent = jnp.broadcast_to(value.reshape(1, 1, 1), (size, 1, 1))
        return jnp.sum(lax.all_to_all(sent, axis, 0, 0, tiled=True))

    total = sum_over(sum_over(local, "fsdp", owners), "grp", groups)
    count = float(groups * owners * order * order)
    clip = CLIP_RMS / jnp.sqrt(total / count + 1e-06)

    gram_part = call(
        gram_kernel,
        shape((2, order, order), F32),
        [VMEM, VMEM],
        VMEM,
        flops=8 * cube,
        moved=14 * order * order,
    )(block, basis_t)

    wide = pltpu.VMEM((2, order, order), F32)
    small = pltpu.VMEM((2, NB, NB), F32)
    update, row_next, col_next = call(
        main_kernel,
        (shape((order, order), BF16), shape((1, order), F32), shape((1, order), F32)),
        [SMEM] + [VMEM] * 5,
        (VMEM, VMEM, VMEM),
        [wide, wide, small, small, small, pltpu.VMEM((2, order, order), BF16)],
        flops=40 * cube,
        moved=20 * order * order,
    )(clip.reshape(1, 1), block, stat_part, gram_part, row_moment[0], col_moment[0])

    pieces = update.reshape(owners, my_rows, order)
    returned = lax.all_to_all(pieces, "fsdp", split_axis=0, concat_axis=0, tiled=True)
    placed = call(
        place_kernel,
        shape((my_rows, owners * order), BF16),
        [SMEM, VMEM],
        VMEM,
        moved=4 * owners * my_rows * order,
    )(table, returned)
    return (placed[None], row_next[None], col_next[None])


def solution(mesh):
    in_specs = (
        P("grp", "fsdp", None),
        P("grp", None),
        P("grp", "fsdp", None, None),
        P("grp", "fsdp", None, None),
        P("grp", "fsdp", None, None),
        P("grp", "fsdp", None, None),
        P("grp", "fsdp", None),
        P("grp", "fsdp", None),
    )
    out_specs = (P("grp", "fsdp", None), P("grp", "fsdp", None), P("grp", "fsdp", None))
    return jax.shard_map(shards, mesh=mesh, in_specs=in_specs, out_specs=out_specs, check_vma=False)
```

time: 432 us -> 136 us (0.31)
  other arithmetic: 253 us -> 1.28 us
  blocking collectives: 0 us -> 70.5 us
  matrix products: 39.8 us -> 0 us
  waiting for transfers between devices: 48.5 us -> 10.1 us
  Pallas kernels: 0 us -> 37.5 us
  starting transfers between devices: 39.8 us -> 5.43 us
  local copies, waits for them, and re-layouts: 37.8 us -> 9.37 us
  between operations: 8.01 us -> 1.41 us
    another operation x33 -> x0, other arithmetic: 243 us -> none  [the longest x28 162 us: refresh(): factor = jnp.linalg.cholesky(inner)]
    all_to_all x0 -> x3, blocking collectives: none -> 70.5 us  [the longest x2 50.5 us: sum_over(): return jnp.sum(lax.all_to_all(sent, axis, 0, 0, tiled=True))]
    all_to_all x4 -> x1, waiting for transfers between devices: 48.5 us -> 10.1 us  [shards(): lax.all_to_all(outgoing, 'fsdp', split_axis=0, concat_axis=0, tiled=True)]
    pallas_call x0 -> x5, Pallas kernels: none -> 37.5 us  [the longest x1 31.6 us: shards(): call(main_kernel, (shape((order, order), BF16), shape((1, order), F32), s...]
    all_to_all x4 -> x1, starting transfers between devices: 39.8 us -> 5.43 us  [shards(): lax.all_to_all(outgoing, 'fsdp', split_axis=0, concat_axis=0, tiled=True)]
    another operation x26 -> x0, matrix products: 28.4 us -> none  [the longest x14 15.7 us: refresh(): ortho = jax.scipy.linalg.solve_triangular(factor, product.T, lower=True).T]
    another operation x36 -> x0, local copies, waits for them, and re-layouts: 24.2 us -> none  [the longest x27 23 us: refresh(): ortho = jax.scipy.linalg.solve_triangular(factor, product.T, lower=True).T]
    dot_general x8 -> x0, matrix products: 11.4 us -> none  [the longest x2 3.71 us: refresh(): inner = jnp.dot(product.T, product, precision=lax.Precision.HIGHEST)]
  transfers between devices with their start and end apart: 4 -> 1, of which waited for: 4 -> 1; matrix products, arithmetic and copies ran while one was open for 1% -> 0% of each run, Pallas kernels for 0% -> 1%
where the time goes in v1:
time: 136 us
  blocking collectives  70.5 us (52%)
  Pallas kernels  37.5 us (28%)
  waiting for transfers between devices  10.1 us (7%)
  local copies, waits for them, and re-layouts  9.37 us (7%)
  starting transfers between devices  5.43 us (4%)
  between operations  1.41 us (1%)
    all_to_all x2, blocking collectives, sum_over(): return jnp.sum(lax.all_to_all(sent, axis, 0, 0, tiled=True))  50.5 us
    pallas_call x1, Pallas kernels, shards(): call(main_kernel, (shape((order, order), BF16), shape((1, order), F32), s...  31.6 us
    all_to_all x1, blocking collectives, shards(): lax.all_to_all(pieces, 'fsdp', split_axis=0, concat_axis=0, tiled=True)  20 us
    all_to_all x1, waiting for transfers between devices, shards(): lax.all_to_all(outgoing, 'fsdp', split_axis=0, concat_axis=0, tiled=True)  10.1 us
    unnamed x22, local copies, waits for them, and re-layouts  8.05 us
    all_to_all x1, starting transfers between devices, shards(): lax.all_to_all(outgoing, 'fsdp', split_axis=0, concat_axis=0, tiled=True)  5.43 us
  transfers between devices with their start and end apart: 1, of which 1 were waited for; matrix products, arithmetic and copies ran while one was open for 0% of the time, Pallas kernels for 1%

profile of v1, /device:TPU:1, one launch (start us, length us, event | category | flops | bytes accessed | tf_op | source)
XLA Modules:
  0.0 135.5 jit_solution(9909249167513991890)
XLA Ops:
  0.6 0.0 copy-start
  0.6 1.0 copy-done
  1.7 0.0 copy-start.5
  1.7 0.7 copy-done.5
  2.3 1.4 %shard_map.103 = (bf16[16,32,512]{2,1,0:T(8,128)(2,1)}, f32[1,1]{1,0:T(1,128)}) custom-call(s32[1,16]{1,0:T(1,128)S(1)} %copy-done.5, bf16[32,8192]{1,0:T(8,128)(2,1)S(1)} %bitcast.14), custom_call_target="tpu_custom_call" | custom-call | bytes 1048576 | tf_op jit(solution)/shard_map/pallas_call | solution.py:211
  3.7 0.7 broadcast_in_dim.22
  4.4 23.6 %all_to_all.20 = f32[16,1,1]{2,1,0:T(1,128)S(1)} all-to-all(f32[16,1,1]{2,1,0:T(1,128)S(1)} %broadcast_in_dim.22), channel_id=1, replica_groups=mesh['fsdp'=16,'grp'=64] {'fsdp'}, dimensions={0} | all-to-all | bytes 128 | tf_op jit(solution)/shard_map/all_to_all | solution.py:231
  28.0 0.6 reduce_sum.18
  28.6 0.7 broadcast_in_dim.23
  29.3 26.9 %all_to_all.21 = f32[64,1,1]{2,1,0:T(1,128)S(1)} all-to-all(f32[64,1,1]{2,1,0:T(1,128)S(1)} %broadcast_in_dim.23), channel_id=1, replica_groups=mesh['fsdp'=16,'grp'=64] {'grp'}, dimensions={0} | all-to-all | bytes 512 | tf_op jit(solution)/shard_map/all_to_all | solution.py:231
  56.2 5.4 %all-to-all-start.2 = ((bf16[16,32,512]{2,1,0:T(8,128)(2,1)}), bf16[16,32,512]{2,1,0:T(8,128)(2,1)S(1)}, u32[]{:S(2)}, u32[]{:S(2)}) async-start(bf16[16,32,512]{2,1,0:T(8,128)(2,1)} %get-tuple-element.11), calls=%async_computation.2 | async-start | bytes 1048576 | tf_op jit(solution)/shard_map/all_to_all | solution.py:218
  61.6 0.0 copy-start.1
  61.6 1.0 copy-done.1
  62.6 0.0 copy-start.2
  62.6 1.0 copy-done.2
  63.7 0.0 copy-start.3
  63.7 1.0 copy-done.3
  64.7 1.0 copy-done.4
  65.8 0.7 shard_map.104
  66.5 0.0 copy-start.7
  66.5 1.0 copy-done.7
  67.5 0.7 reduce_sum.19
  68.8 10.1 %all-to-all-done.2 = bf16[16,32,512]{2,1,0:T(8,128)(2,1)S(1)} async-done(((bf16[16,32,512]{2,1,0:T(8,128)(2,1)}), bf16[16,32,512]{2,1,0:T(8,128)(2,1)S(1)}, u32[]{:S(2)}, u32[]{:S(2)}) %all-to-all-start.2) | async-done | bytes 524320 | tf_op jit(solution)/shard_map/all_to_all | solution.py:218
  78.9 1.2 copy-done.8
  80.2 2.3 %shard_map.105.gram_part = f32[2,512,512]{2,1,0:T(8,128)S(1)} custom-call(bf16[512,512]{1,0:T(8,128)(2,1)S(1)} %bitcast.15, bf16[2,512,512]{2,1,0:T(8,128)(2,1)S(1)} %copy-done.8), custom_call_target="tpu_custom_call" | custom-call | flops 2147483648 | bytes 3670016 | tf_op jit(solution)/shard_map/pallas_call | solution.py:237
  82.5 0.0 copy-done.9
  82.5 0.0 copy-done.10
  82.5 0.0 copy-start.6
  82.5 31.6 %shard_map.106 = (bf16[512,512]{1,0:T(8,128)(2,1)S(1)}, f32[1,512]{1,0:T(1,128)}, f32[1,512]{1,0:T(1,128)}) custom-call(f32[1,1]{1,0:T(1,128)} %bitcast.2.clip_ref, bf16[512,512]{1,0:T(8,128)(2,1)S(1)} %bitcast.16, f32[2,512,512]{2,1,0:T(8,128)S(1)} %get-tuple-element.12.stat_part, f32[2,512,512]{2,1,0:T(8,128)S(1)} %shard_map.105.gram_part, ...), custom_call_target="tpu_custom_call" | custom-call | flops 10737418240 | bytes 5242880 | tf_op jit(solution)/shard_map/pallas_call | solution.py:248
  114.1 20.0 %all_to_all.22.back_ref = bf16[16,32,512]{2,1,0:T(8,128)(2,1)S(1)} all-to-all(bf16[16,32,512]{2,1,0:T(8,128)(2,1)S(1)} %bitcast.17), channel_id=1, replica_groups=mesh['fsdp'=16,'grp'=64] {'fsdp'}, dimensions={0} | all-to-all | bytes 1048576 | tf_op jit(solution)/shard_map/all_to_all | solution.py:259
  134.2 0.0 copy-done.6
  134.2 1.4 %shard_map.107 = bf16[32,8192]{1,0:T(8,128)(2,1)} custom-call(s32[1,16]{1,0:T(1,128)S(1)} %copy-done.6, bf16[16,32,512]{2,1,0:T(8,128)(2,1)S(1)} %all_to_all.22.back_ref), custom_call_target="tpu_custom_call" | custom-call | bytes 1048576 | tf_op jit(solution)/shard_map/pallas_call | solution.py:260
  (4 shorter events, 0.0 us)
Async XLA Ops:
  0.6 1.0 copy-start
  1.7 0.7 copy-start.5
  56.2 22.8 %all-to-all-start.2 = ((bf16[16,32,512]{2,1,0:T(8,128)(2,1)}), bf16[16,32,512]{2,1,0:T(8,128)(2,1)S(1)}, u32[]{:S(2)}, u32[]{:S(2)}) async-start(bf16[16,32,512]{2,1,0:T(8,128)(2,1)} %get-tuple-element.11), calls=%async_computation.2 | async-start | bytes 1048576 | tf_op jit(solution)/shard_map/all_to_all | solution.py:218
  61.6 1.0 copy-start.1
  62.6 1.0 copy-start.2
  63.7 1.0 copy-start.3
  64.7 1.0 copy-start.4
  66.5 1.0 copy-start.7
  78.9 1.2 copy-start.8
  80.2 2.3 %copy-start.9 = (f32[1,1,512]{2,1,0:T(1,128)S(1)}, f32[1,1,512]{2,1,0:T(1,128)}, u32[]{:S(2)}) copy-start(f32[1,1,512]{2,1,0:T(1,128)} %param.14) | copy-start | bytes 6148
  80.2 2.4 %copy-start.10 = (f32[1,1,512]{2,1,0:T(1,128)S(1)}, f32[1,1,512]{2,1,0:T(1,128)}, u32[]{:S(2)}) copy-start(f32[1,1,512]{2,1,0:T(1,128)} %param.15) | copy-start | bytes 6148
  82.5 51.6 %copy-start.6 = (s32[1,16]{1,0:T(1,128)S(1)}, s32[1,16]{1,0:T(1,128)}, u32[]{:S(2)}) copy-start(s32[1,16]{1,0:T(1,128)} %table_ref.3) | copy-start | bytes 196

commit v2 on v1

--- a/solution.py
+++ b/solution.py
@@ -1,3 +1,5 @@
+import functools
+
 import jax
 import jax.numpy as jnp
 from jax import lax
@@ -14,6 +16,7 @@
 TILE = 8
 NB = 128
 NT = NB // TILE
+EXTRA = 16
 NN = (((1,), (0,)), ((), ()))
 NT_DIMS = (((1,), (1,)), ((), ()))
 TN = (((0,), (0,)), ((), ()))
@@ -48,7 +51,7 @@
     return jnp.broadcast_to(x[r : r + 1, :], (TILE, NB))
 
 
-def factor_steps(get, aug, side, out):
+def factor_steps(get, aug, side, out, slot):
     lanes = lax.broadcasted_iota(jnp.int32, (TILE, NB), 1)
     subs = lax.broadcasted_iota(jnp.int32, (TILE, NB), 0)
 
@@ -78,7 +81,7 @@
             forward = forward - below * both_row
             yield
         inverse = 1.0 / pivots
-        out[at(k)] = forward * lax.rsqrt(pivots)
+        out[slot + side, TILE * k : TILE * k + TILE, :] = forward * lax.rsqrt(pivots)
         tile = tile * inverse
         both = both * inverse
         tile_rows = [row(tile, j) for j in range(TILE)]
@@ -96,21 +99,40 @@
         yield
 
 
-def interleave(steps):
-    steps = list(steps)
-    while steps:
+def interleave(steps, later, every):
+    steps, later, count = list(steps), list(later), 0
+    while steps or later:
         steps = [s for s in steps if next(s, steps) is not steps]
-
-
-def prep_kernel(table_ref, grad_ref, out_ref, sum_ref):
-    owners, my_rows, order = out_ref.shape
+        count += 1
+        if count % every == 0 or not steps:
+            later = [s for s in later if next(s, later) is not later]
+
+
+def prep_kernel(table_ref, grad_ref, out_ref):
+    owners, _, width = out_ref.shape
+    my_rows = grad_ref.shape[0]
+    order = grad_ref.shape[1] // owners
     total = jnp.zeros((my_rows, order), F32)
     for j in range(owners):
         part = grad_ref[:, j * order : (j + 1) * order]
-        out_ref[table_ref[0, j]] = part
+        for c in range(order // width):
+            out_ref[table_ref[0, j], c * my_rows : (c + 1) * my_rows, :] = part[:, c * width : (c + 1) * width]
         wide = part.astype(F32)
         total = total + wide * wide
-    sum_ref[...] = jnp.sum(total).reshape(1, 1)
+    high, mid, low = split3(jnp.broadcast_to(jnp.sum(total).reshape(1, 1), (EXTRA, width)))
+    rows = lax.broadcasted_iota(jnp.int32, (EXTRA, width), 0)
+    extra = jnp.where(rows == 0, high.astype(F32), jnp.where(rows == 1, mid.astype(F32), low.astype(F32)))
+    extra = jnp.where(rows < 3, extra, 0.0).astype(BF16)
+    for o in range(owners):
+        out_ref[o, order // width * my_rows :, :] = extra
+
+
+def sum_kernel(block_ref, sum_ref):
+    owners, height, width = block_ref.shape
+    total = jnp.zeros((EXTRA, width), F32)
+    for o in range(owners):
+        total = total + block_ref[o, height - EXTRA :, :].astype(F32)
+    sum_ref[...] = jnp.broadcast_to(jnp.sum(total, axis=0).reshape(1, 1, width), sum_ref.shape)
 
 
 def place_kernel(table_ref, back_ref, out_ref):
@@ -126,44 +148,82 @@
         stat_part[side] = DECAY_STAT * mm(turned, stat[...])
 
 
-def gram_kernel(block_ref, basis_t, gram_part):
+def gram_kernel(recv_ref, basis_t, block_ref, gram_part):
+    owners, height, width = recv_ref.shape
+    order = block_ref.shape[0]
+    my_rows = order // owners
+    for o in range(owners):
+        for c in range(order // width):
+            piece = recv_ref[o, c * my_rows : (c + 1) * my_rows, :]
+            block_ref[o * my_rows : (o + 1) * my_rows, c * width : (c + 1) * width] = piece
     block = block_ref[...]
     gram_part[0] = (1.0 - DECAY_STAT) * mm_split(mm(basis_t[0], block), block, NT_DIMS)
     gram_part[1] = (1.0 - DECAY_STAT) * mm_split(mm(basis_t[1], block, NT_DIMS), block)
 
 
 def main_kernel(
-    clip_ref, block_ref, stat_part, gram_part, row_ref, col_ref, update_ref, row_out, col_out,
-    s_ref, a_ref, t_ref, aug_ref, w_ref, q_ref,
+    count, sum_ref, block_ref, stat_part, gram_part, row_ref, col_ref, update_ref, row_out, col_out,
+    s_ref, a_ref, t_ref, aug_ref, w_ref, p_ref, q_ref,
 ):
     order = block_ref.shape[0]
-    clip = clip_ref[0, 0]
+    blocks = order // NB
+    total = jnp.sum(jnp.sum(sum_ref[...], axis=0), axis=1, keepdims=True) * (1.0 / sum_ref.shape[2])
+    clip = CLIP_RMS / jnp.sqrt(total / count + 1e-06)
     for side in range(2):
         a = stat_part[side] + (clip * clip) * gram_part[side]
         a_ref[side] = a
         high, mid, low = split3(a)
-        for k in range(order // NB):
+        for k in range(blocks):
             part = slice(k * NB, order)
             mine = slice(k * NB, (k + 1) * NB)
-            total = mm(low[mine], high[part], NT_DIMS) + mm(high[mine], low[part], NT_DIMS)
-            total = total + mm(mid[mine], mid[part], NT_DIMS)
-            total = total + mm(mid[mine], high[part], NT_DIMS) + mm(high[mine], mid[part], NT_DIMS)
-            s_ref[side, mine, part] = total + mm(high[mine], high[part], NT_DIMS)
-
-    for k in range(order // NB):
-        mine = slice(k * NB, (k + 1) * NB)
+            near = mm(low[mine], high[part], NT_DIMS) + mm(high[mine], low[part], NT_DIMS)
+            near = near + mm(mid[mine], mid[part], NT_DIMS)
+            near = near + mm(mid[mine], high[part], NT_DIMS) + mm(high[mine], mid[part], NT_DIMS)
+            s_ref[side, mine, part] = near + mm(high[mine], high[part], NT_DIMS)
+
+    def at(k):
+        return slice(k * NB, (k + 1) * NB)
+
+    def finish(k, side):
+        w = w_ref[k % 2 * 2 + side]
+        rest = slice((k + 1) * NB, order)
+        if k + 2 < blocks:
+            far = slice((k + 2) * NB, order)
+            p_ref[side, :, far] = mm_full(w, s_ref[side, at(k), far])
+            yield
+        if k + 1 < blocks:
+            panel_t = p_ref[side, :, rest].T
+        half = order // 2
+        for c in range(2):
+            cols = slice(c * half, (c + 1) * half)
+            turned = mm_full(w, a_ref[side, at(k), cols])
+            q_ref[side, at(k), cols] = turned.astype(BF16)
+            yield
+            if k + 1 < blocks:
+                a_ref[side, rest, cols] = a_ref[side, rest, cols] - mm_full(panel_t, turned)
+                yield
+        for i in range(k + 1, blocks):
+            first = max(i, k + 2)
+            if first < blocks:
+                cols = slice(first * NB, order)
+                panel_i = panel_t[(i - k - 1) * NB : (i - k) * NB]
+                s_ref[side, at(i), cols] = s_ref[side, at(i), cols] - mm_full(panel_i, p_ref[side, :, cols])
+                yield
+
+    waiting = []
+    for k in range(blocks):
+        slot = k % 2 * 2
         for side in range(2):
-            t_ref[side] = s_ref[side, mine, mine]
-        interleave([factor_steps(t_ref, aug_ref, side, w_ref) for side in range(2)])
-        for side in range(2):
-            turned = mm_full(w_ref[side], a_ref[side, mine, :])
-            q_ref[side, mine, :] = turned.astype(BF16)
-            if (k + 1) * NB < order:
-                rest = slice((k + 1) * NB, order)
-                panel = mm_full(w_ref[side], s_ref[side, mine, rest])
-                panel_t = panel.T
-                s_ref[side, rest, rest] = s_ref[side, rest, rest] - mm_full(panel_t, panel)
-                a_ref[side, rest, :] = a_ref[side, rest, :] - mm_full(panel_t, turned)
+            if k == 0:
+                t_ref[side] = s_ref[side, at(0), at(0)]
+        interleave([factor_steps(t_ref, aug_ref, side, w_ref, slot) for side in range(2)], waiting, 8)
+        if k + 1 < blocks:
+            for side in range(2):
+                panel = mm_full(w_ref[slot + side], s_ref[side, at(k), at(k + 1)])
+                p_ref[side, :, at(k + 1)] = panel
+                t_ref[side] = s_ref[side, at(k + 1), at(k + 1)] - mm_full(panel.T, panel)
+        waiting = [finish(k, side) for side in range(2)]
+    interleave([], waiting, 1)
 
     block = block_ref[...]
     left_t = q_ref[0]
@@ -188,14 +248,14 @@
 SMEM = pl.BlockSpec(memory_space=pltpu.SMEM)
 
 
-def call(kernel, out_shapes, in_specs, out_specs, scratch=(), flops=0, moved=0):
+def call(kernel, out_shapes, in_specs, out_specs, scratch=(), flops=0, moved=0, limit=12):
     return pl.pallas_call(
         kernel,
         out_shape=out_shapes,
         in_specs=in_specs,
         out_specs=out_specs,
         scratch_shapes=list(scratch),
-        compiler_params=pltpu.CompilerParams(vmem_limit_bytes=48 * 2**20),
+        compiler_params=pltpu.CompilerParams(vmem_limit_bytes=limit * 2**20),
         cost_estimate=pl.CostEstimate(flops=flops, bytes_accessed=moved, transcendentals=0),
     )
 
@@ -208,14 +268,14 @@
     shape = jax.ShapeDtypeStruct
     cube = 2 * order**3
 
-    outgoing, local = call(
+    outgoing = call(
         prep_kernel,
-        (shape((owners, my_rows, order), BF16), shape((1, 1), F32)),
+        shape((owners, order // NB * my_rows + EXTRA, NB), BF16),
         [SMEM, VMEM],
-        (VMEM, VMEM),
+        VMEM,
         moved=4 * owners * my_rows * order,
     )(table, grad[0])
-    block = lax.all_to_all(outgoing, "fsdp", split_axis=0, concat_axis=0, tiled=True).reshape(order, order)
+    received = lax.all_to_all(outgoing, "fsdp", split_axis=0, concat_axis=0, tiled=True)
 
     basis_t, stat_part = call(
         early_kernel,
@@ -226,34 +286,30 @@
         moved=16 * order * order,
     )(left_stat[0, 0], right_stat[0, 0], left_basis[0, 0], right_basis[0, 0])
 
-    def sum_over(value, axis, size):
-        sent = jnp.broadcast_to(value.reshape(1, 1, 1), (size, 1, 1))
-        return jnp.sum(lax.all_to_all(sent, axis, 0, 0, tiled=True))
-
-    total = sum_over(sum_over(local, "fsdp", owners), "grp", groups)
-    count = float(groups * owners * order * order)
-    clip = CLIP_RMS / jnp.sqrt(total / count + 1e-06)
-
-    gram_part = call(
+    mine = call(sum_kernel, shape((groups, 1, NB), F32), [VMEM], VMEM, moved=64 * owners * NB)(received)
+    sums = lax.all_to_all(mine, "grp", split_axis=0, concat_axis=0, tiled=True)
+
+    block, gram_part = call(
         gram_kernel,
-        shape((2, order, order), F32),
+        (shape((order, order), BF16), shape((2, order, order), F32)),
         [VMEM, VMEM],
-        VMEM,
+        (VMEM, VMEM),
         flops=8 * cube,
         moved=14 * order * order,
-    )(block, basis_t)
+    )(received, basis_t)
 
     wide = pltpu.VMEM((2, order, order), F32)
     small = pltpu.VMEM((2, NB, NB), F32)
     update, row_next, col_next = call(
-        main_kernel,
+        functools.partial(main_kernel, float(groups * owners * order * order)),
         (shape((order, order), BF16), shape((1, order), F32), shape((1, order), F32)),
-        [SMEM] + [VMEM] * 5,
+        [VMEM] * 6,
         (VMEM, VMEM, VMEM),
-        [wide, wide, small, small, small, pltpu.VMEM((2, order, order), BF16)],
+        [wide, wide, small, small, pltpu.VMEM((4, NB, NB), F32), pltpu.VMEM((2, NB, order), F32), pltpu.VMEM((2, order, order), BF16)],
         flops=40 * cube,
         moved=20 * order * order,
-    )(clip.reshape(1, 1), block, stat_part, gram_part, row_moment[0], col_moment[0])
+        limit=24,
+    )(sums, block, stat_part, gram_part, row_moment[0], col_moment[0])
 
     pieces = update.reshape(owners, my_rows, order)
     returned = lax.all_to_all(pieces, "fsdp", split_axis=0, concat_axis=0, tiled=True)

time: 136 us -> 120 us (0.88)
  blocking collectives: 70.5 us -> 21.5 us
  starting transfers between devices: 5.43 us -> 30.6 us
  waiting for transfers between devices: 10.1 us -> 23.9 us
  Pallas kernels: 37.5 us -> 35.3 us
    all_to_all x2 -> x0, blocking collectives: 50.5 us -> none  [sum_over(): return jnp.sum(lax.all_to_all(sent, axis, 0, 0, tiled=True))]
    all_to_all x0 -> x1, starting transfers between devices: none -> 13.1 us  [shards(): sums = lax.all_to_all(mine, 'grp', split_axis=0, concat_axis=0, tiled=True)]
    all_to_all x1, starting transfers between devices: 5.43 us -> 17.5 us  [shards(): lax.all_to_all(outgoing, 'fsdp', split_axis=0, concat_axis=0, tiled=True)]
    all_to_all x0 -> x1, waiting for transfers between devices: none -> 8.32 us  [shards(): sums = lax.all_to_all(mine, 'grp', split_axis=0, concat_axis=0, tiled=True)]
    all_to_all x1, waiting for transfers between devices: 10.1 us -> 15.5 us  [shards(): lax.all_to_all(outgoing, 'fsdp', split_axis=0, concat_axis=0, tiled=True)]
    pallas_call x3 -> x4, Pallas kernels: 35.3 us -> 33.1 us  [the longest x1 28.5 us: shards(): call(functools.partial(main_kernel, float(groups * owners * order * order...]
    all_to_all x1, blocking collectives: 20 us -> 21.5 us  [shards(): lax.all_to_all(pieces, 'fsdp', split_axis=0, concat_axis=0, tiled=True)]
    unnamed x22 -> x30, local copies, waits for them, and re-layouts: 8.05 us -> 8.12 us
  transfers between devices with their start and end apart: 1 -> 2, of which waited for: 1 -> 2; matrix products, arithmetic and copies ran while one was open for 0% -> 0% of each run, Pallas kernels for 1% -> 3%
where the time goes in v2:
time: 120 us
  Pallas kernels  35.3 us (29%)
  starting transfers between devices  30.6 us (26%)
  waiting for transfers between devices  23.9 us (20%)
  blocking collectives  21.5 us (18%)
  local copies, waits for them, and re-layouts  8.12 us (7%)
    pallas_call x1, Pallas kernels, shards(): call(functools.partial(main_kernel, float(groups * owners * order * order...  28.5 us
    all_to_all x1, blocking collectives, shards(): lax.all_to_all(pieces, 'fsdp', split_axis=0, concat_axis=0, tiled=True)  21.5 us
    all_to_all x1, starting transfers between devices, shards(): lax.all_to_all(outgoing, 'fsdp', split_axis=0, concat_axis=0, tiled=True)  17.5 us
    all_to_all x1, waiting for transfers between devices, shards(): lax.all_to_all(outgoing, 'fsdp', split_axis=0, concat_axis=0, tiled=True)  15.5 us
    all_to_all x1, starting transfers between devices, shards(): sums = lax.all_to_all(mine, 'grp', split_axis=0, concat_axis=0, tiled=True)  13.1 us
    all_to_all x1, waiting for transfers between devices, shards(): sums = lax.all_to_all(mine, 'grp', split_axis=0, concat_axis=0, tiled=True)  8.32 us
    unnamed x30, local copies, waits for them, and re-layouts  8.12 us
  transfers between devices with their start and end apart: 2, of which 2 were waited for; matrix products, arithmetic and copies ran while one was open for 0% of the time, Pallas kernels for 3%

profile of v2, /device:TPU:1, one launch (start us, length us, event | category | flops | bytes accessed | tf_op | source)
XLA Modules:
  0.0 120.0 jit_solution(18249290071335218940)
XLA Ops:
  0.6 0.0 copy-start
  0.6 1.0 copy-done
  1.7 0.0 copy-start.5
  1.7 0.7 copy-done.5
  2.3 1.6 %shard_map.103 = bf16[16,144,128]{2,1,0:T(8,128)(2,1)} custom-call(s32[1,16]{1,0:T(1,128)S(1)} %copy-done.5, bf16[32,8192]{1,0:T(8,128)(2,1)S(1)} %bitcast.11), custom_call_target="tpu_custom_call" | custom-call | bytes 1048576 | tf_op jit(solution)/shard_map/pallas_call | solution.py:271
  4.0 17.5 %all-to-all-start = ((bf16[16,144,128]{2,1,0:T(8,128)(2,1)}), bf16[16,144,128]{2,1,0:T(8,128)(2,1)S(1)}, u32[]{:S(2)}, u32[]{:S(2)}) async-start(bf16[16,144,128]{2,1,0:T(8,128)(2,1)} %shard_map.103), calls=%async_computation | async-start | bytes 1179648 | tf_op jit(solution)/shard_map/all_to_all | solution.py:278
  21.5 0.0 copy-done.1
  21.5 0.0 copy-done.2
  21.5 0.0 copy-done.3
  21.5 0.0 copy-done.4
  21.5 0.7 shard_map.105
  22.3 0.0 copy-start.7
  22.3 1.3 %copy-done.7 = f32[2,512,512]{2,1,0:T(8,128)} copy-done((f32[2,512,512]{2,1,0:T(8,128)}, f32[2,512,512]{2,1,0:T(8,128)S(1)}, u32[]{:S(2)}) %copy-start.7) | copy-done | bytes 2097176
  23.6 1.0 copy-done.9
  24.6 15.5 %all-to-all-done.block_ref.recv_ref = bf16[16,144,128]{2,1,0:T(8,128)(2,1)S(1)} async-done(((bf16[16,144,128]{2,1,0:T(8,128)(2,1)}), bf16[16,144,128]{2,1,0:T(8,128)(2,1)S(1)}, u32[]{:S(2)}, u32[]{:S(2)}) %all-to-all-start) | async-done | bytes 589856 | tf_op jit(solution)/shard_map/all_to_all | solution.py:278
  40.1 0.7 shard_map.104
  40.8 13.1 %all-to-all-start.1 = ((f32[64,1,128]{2,1,0:T(1,128)}), f32[64,1,128]{2,1,0:T(1,128)S(1)}, u32[]{:S(2)}, u32[]{:S(2)}) async-start(f32[64,1,128]{2,1,0:T(1,128)} %shard_map.104), calls=%async_computation.1 | async-start | bytes 65536 | tf_op jit(solution)/shard_map/all_to_all | solution.py:290
  53.8 0.0 copy-start.10
  53.9 1.2 %copy-done.10 = bf16[2,512,512]{2,1,0:T(8,128)(2,1)S(1)} copy-done((bf16[2,512,512]{2,1,0:T(8,128)(2,1)S(1)}, bf16[2,512,512]{2,1,0:T(8,128)(2,1)}, u32[]{:S(2)}) %copy-start.10) | copy-done | bytes 1048600
  55.1 2.4 %shard_map.106 = (bf16[512,512]{1,0:T(8,128)(2,1)S(1)}, f32[2,512,512]{2,1,0:T(8,128)S(1)}) custom-call(bf16[16,144,128]{2,1,0:T(8,128)(2,1)S(1)} %all-to-all-done.block_ref.recv_ref, bf16[2,512,512]{2,1,0:T(8,128)(2,1)S(1)} %copy-done.10), custom_call_target="tpu_custom_call" | custom-call | flops 2147483648 | bytes 3670016 | tf_op jit(solution)/shard_map/pallas_call | solution.py:292
  57.5 0.0 copy-start.13
  57.5 1.3 %copy-done.13 = f32[2,512,512]{2,1,0:T(8,128)} copy-done((f32[2,512,512]{2,1,0:T(8,128)}, f32[2,512,512]{2,1,0:T(8,128)S(1)}, u32[]{:S(2)}) %copy-start.13) | copy-done | bytes 2097176
  58.8 8.3 %all-to-all-done.1.sum_ref = f32[64,1,128]{2,1,0:T(1,128)S(1)} async-done(((f32[64,1,128]{2,1,0:T(1,128)}), f32[64,1,128]{2,1,0:T(1,128)S(1)}, u32[]{:S(2)}, u32[]{:S(2)}) %all-to-all-start.1) | async-done | bytes 32800 | tf_op jit(solution)/shard_map/all_to_all | solution.py:290
  67.1 0.0 copy-done.8
  67.1 0.0 copy-done.11
  67.1 0.0 copy-done.12
  67.1 0.0 copy-start.14
  67.1 1.6 %copy-done.14 = f32[2,512,512]{2,1,0:T(8,128)S(1)} copy-done((f32[2,512,512]{2,1,0:T(8,128)S(1)}, f32[2,512,512]{2,1,0:T(8,128)}, u32[]{:S(2)}) %copy-start.14) | copy-done | bytes 2097176
  68.7 28.5 %shard_map.107 = (bf16[512,512]{1,0:T(8,128)(2,1)S(1)}, f32[1,512]{1,0:T(1,128)}, f32[1,512]{1,0:T(1,128)}) custom-call(f32[64,1,128]{2,1,0:T(1,128)S(1)} %all-to-all-done.1.sum_ref, bf16[512,512]{1,0:T(8,128)(2,1)S(1)} %get-tuple-element.11.block_ref, f32[2,512,512]{2,1,0:T(8,128)S(1)} %copy-done.8, f32[2,512,512]{2,1,0:T(8,128)S(1)} %copy-done.14, ...), custom_call_target="tpu_custom_call" | custom-call | flops 10737418240 | bytes 5242880 | tf_op jit(solution)/shard_map/pallas_call | solution.py:303
  97.2 21.5 %all_to_all.15.back_ref = bf16[16,32,512]{2,1,0:T(8,128)(2,1)S(1)} all-to-all(bf16[16,32,512]{2,1,0:T(8,128)(2,1)S(1)} %bitcast.12), channel_id=1, replica_groups=mesh['fsdp'=16,'grp'=64] {'fsdp'}, dimensions={0} | all-to-all | bytes 1048576 | tf_op jit(solution)/shard_map/all_to_all | solution.py:315
  118.7 0.0 copy-done.6
  118.7 1.4 %shard_map.108 = bf16[32,8192]{1,0:T(8,128)(2,1)} custom-call(s32[1,16]{1,0:T(1,128)S(1)} %copy-done.6, bf16[16,32,512]{2,1,0:T(8,128)(2,1)S(1)} %all_to_all.15.back_ref), custom_call_target="tpu_custom_call" | custom-call | bytes 1048576 | tf_op jit(solution)/shard_map/pallas_call | solution.py:316
  (9 shorter events, 0.0 us)
Async XLA Ops:
  0.6 1.0 copy-start
  1.7 0.7 copy-start.5
  2.3 19.1 %copy-start.1 = (bf16[1,1,512,512]{3,2,1,0:T(8,128)(2,1)S(1)}, bf16[1,1,512,512]{3,2,1,0:T(8,128)(2,1)}, u32[]{:S(2)}) copy-start(bf16[1,1,512,512]{3,2,1,0:T(8,128)(2,1)} %param.10) | copy-start | bytes 1572868
  2.3 19.2 %copy-start.2 = (bf16[1,1,512,512]{3,2,1,0:T(8,128)(2,1)S(1)}, bf16[1,1,512,512]{3,2,1,0:T(8,128)(2,1)}, u32[]{:S(2)}) copy-start(bf16[1,1,512,512]{3,2,1,0:T(8,128)(2,1)} %param.11) | copy-start | bytes 1572868
  2.3 19.2 %copy-start.3 = (bf16[1,1,512,512]{3,2,1,0:T(8,128)(2,1)S(1)}, bf16[1,1,512,512]{3,2,1,0:T(8,128)(2,1)}, u32[]{:S(2)}) copy-start(bf16[1,1,512,512]{3,2,1,0:T(8,128)(2,1)} %param.12) | copy-start | bytes 1572868
  2.3 19.2 %copy-start.4 = (bf16[1,1,512,512]{3,2,1,0:T(8,128)(2,1)S(1)}, bf16[1,1,512,512]{3,2,1,0:T(8,128)(2,1)}, u32[]{:S(2)}) copy-start(bf16[1,1,512,512]{3,2,1,0:T(8,128)(2,1)} %param.13) | copy-start | bytes 1572868
  4.0 36.2 %all-to-all-start = ((bf16[16,144,128]{2,1,0:T(8,128)(2,1)}), bf16[16,144,128]{2,1,0:T(8,128)(2,1)S(1)}, u32[]{:S(2)}, u32[]{:S(2)}) async-start(bf16[16,144,128]{2,1,0:T(8,128)(2,1)} %shard_map.103), calls=%async_computation | async-start | bytes 1179648 | tf_op jit(solution)/shard_map/all_to_all | solution.py:278
  22.3 1.3 %copy-start.7 = (f32[2,512,512]{2,1,0:T(8,128)}, f32[2,512,512]{2,1,0:T(8,128)S(1)}, u32[]{:S(2)}) copy-start(f32[2,512,512]{2,1,0:T(8,128)S(1)} %get-tuple-element.12.stat_part) | copy-start | bytes 6291460
  23.6 1.0 copy-start.9
  40.8 26.3 %all-to-all-start.1 = ((f32[64,1,128]{2,1,0:T(1,128)}), f32[64,1,128]{2,1,0:T(1,128)S(1)}, u32[]{:S(2)}, u32[]{:S(2)}) async-start(f32[64,1,128]{2,1,0:T(1,128)} %shard_map.104), calls=%async_computation.1 | async-start | bytes 65536 | tf_op jit(solution)/shard_map/all_to_all | solution.py:290
  53.8 1.2 %copy-start.10 = (bf16[2,512,512]{2,1,0:T(8,128)(2,1)S(1)}, bf16[2,512,512]{2,1,0:T(8,128)(2,1)}, u32[]{:S(2)}) copy-start(bf16[2,512,512]{2,1,0:T(8,128)(2,1)} %copy-done.9) | copy-start | bytes 3145732
  55.1 12.0 %copy-start.8 = (f32[2,512,512]{2,1,0:T(8,128)S(1)}, f32[2,512,512]{2,1,0:T(8,128)}, u32[]{:S(2)}) copy-start(f32[2,512,512]{2,1,0:T(8,128)} %copy-done.7) | copy-start | bytes 6291460
  55.1 12.0 %copy-start.11 = (f32[1,1,512]{2,1,0:T(1,128)S(1)}, f32[1,1,512]{2,1,0:T(1,128)}, u32[]{:S(2)}) copy-start(f32[1,1,512]{2,1,0:T(1,128)} %param.14) | copy-start | bytes 6148
  55.1 12.0 %copy-start.12 = (f32[1,1,512]{2,1,0:T(1,128)S(1)}, f32[1,1,512]{2,1,0:T(1,128)}, u32[]{:S(2)}) copy-start(f32[1,1,512]{2,1,0:T(1,128)} %param.15) | copy-start | bytes 6148
  57.5 1.3 %copy-start.13 = (f32[2,512,512]{2,1,0:T(8,128)}, f32[2,512,512]{2,1,0:T(8,128)S(1)}, u32[]{:S(2)}) copy-start(f32[2,512,512]{2,1,0:T(8,128)S(1)} %get-tuple-element.13.gram_part) | copy-start | bytes 6291460
  67.1 1.6 %copy-start.14 = (f32[2,512,512]{2,1,0:T(8,128)S(1)}, f32[2,512,512]{2,1,0:T(8,128)}, u32[]{:S(2)}) copy-start(f32[2,512,512]{2,1,0:T(8,128)} %copy-done.13) | copy-start | bytes 6291460
  68.7 50.0 %copy-start.6 = (s32[1,16]{1,0:T(1,128)S(1)}, s32[1,16]{1,0:T(1,128)}, u32[]{:S(2)}) copy-start(s32[1,16]{1,0:T(1,128)} %table_ref.3) | copy-start | bytes 196

commit v3 on v2

--- a/solution.py
+++ b/solution.py
@@ -17,6 +17,7 @@
 NB = 128
 NT = NB // TILE
 EXTRA = 16
+CHUNKS = 4
 NN = (((1,), (0,)), ((), ()))
 NT_DIMS = (((1,), (1,)), ((), ()))
 TN = (((0,), (0,)), ((), ()))
@@ -108,13 +109,24 @@
             later = [s for s in later if next(s, later) is not later]
 
 
-def prep_kernel(table_ref, grad_ref, out_ref):
+def prep_kernel(table_hbm, grad_hbm, out_ref, table_ref, grad_ref, table_sem, grad_sem):
     owners, _, width = out_ref.shape
-    my_rows = grad_ref.shape[0]
-    order = grad_ref.shape[1] // owners
+    chunks, my_rows, span = grad_ref.shape
+    order = chunks * span // owners
+    table_copy = pltpu.make_async_copy(table_hbm, table_ref, table_sem)
+    table_copy.start()
+    copies = []
+    for g in range(chunks):
+        part = grad_hbm.at[:, g * span : (g + 1) * span]
+        copies.append(pltpu.make_async_copy(part, grad_ref.at[g], grad_sem.at[g]))
+        copies[g].start()
+    table_copy.wait()
     total = jnp.zeros((my_rows, order), F32)
     for j in range(owners):
-        part = grad_ref[:, j * order : (j + 1) * order]
+        g, first = divmod(j * order, span)
+        if first == 0:
+            copies[g].wait()
+        part = grad_ref[g, :, first : first + order]
         for c in range(order // width):
             out_ref[table_ref[0, j], c * my_rows : (c + 1) * my_rows, :] = part[:, c * width : (c + 1) * width]
         wide = part.astype(F32)
@@ -148,28 +160,42 @@
         stat_part[side] = DECAY_STAT * mm(turned, stat[...])
 
 
-def gram_kernel(recv_ref, basis_t, block_ref, gram_part):
+def gram_kernel(recv_ref, basis_hbm, block_ref, gram_hbm, basis_t, gram_part, in_sem, out_sem):
     owners, height, width = recv_ref.shape
     order = block_ref.shape[0]
     my_rows = order // owners
+    loads = [pltpu.make_async_copy(basis_hbm.at[s], basis_t.at[s], in_sem.at[s]) for s in range(2)]
+    stores = [pltpu.make_async_copy(gram_part.at[s], gram_hbm.at[s], out_sem.at[s]) for s in range(2)]
+    for load in loads:
+        load.start()
     for o in range(owners):
         for c in range(order // width):
             piece = recv_ref[o, c * my_rows : (c + 1) * my_rows, :]
             block_ref[o * my_rows : (o + 1) * my_rows, c * width : (c + 1) * width] = piece
     block = block_ref[...]
+    loads[0].wait()
     gram_part[0] = (1.0 - DECAY_STAT) * mm_split(mm(basis_t[0], block), block, NT_DIMS)
+    stores[0].start()
+    loads[1].wait()
     gram_part[1] = (1.0 - DECAY_STAT) * mm_split(mm(basis_t[1], block, NT_DIMS), block)
+    stores[1].start()
+    for store in stores:
+        store.wait()
 
 
 def main_kernel(
-    count, sum_ref, block_ref, stat_part, gram_part, row_ref, col_ref, update_ref, row_out, col_out,
-    s_ref, a_ref, t_ref, aug_ref, w_ref, p_ref, q_ref,
+    count, sum_ref, block_ref, stat_part, gram_hbm, row_ref, col_ref, update_ref, row_out, col_out,
+    gram_part, gram_sem, s_ref, a_ref, t_ref, aug_ref, w_ref, p_ref, q_ref,
 ):
     order = block_ref.shape[0]
     blocks = order // NB
+    loads = [pltpu.make_async_copy(gram_hbm.at[s], gram_part.at[s], gram_sem.at[s]) for s in range(2)]
+    for load in loads:
+        load.start()
     total = jnp.sum(jnp.sum(sum_ref[...], axis=0), axis=1, keepdims=True) * (1.0 / sum_ref.shape[2])
     clip = CLIP_RMS / jnp.sqrt(total / count + 1e-06)
     for side in range(2):
+        loads[side].wait()
         a = stat_part[side] + (clip * clip) * gram_part[side]
         a_ref[side] = a
         high, mid, low = split3(a)
@@ -246,6 +272,8 @@
 
 VMEM = pl.BlockSpec(memory_space=pltpu.VMEM)
 SMEM = pl.BlockSpec(memory_space=pltpu.SMEM)
+HBM = pl.BlockSpec(memory_space=pltpu.HBM)
+DMA = pltpu.SemaphoreType.DMA
 
 
 def call(kernel, out_shapes, in_specs, out_specs, scratch=(), flops=0, moved=0, limit=12):
@@ -271,8 +299,14 @@
     outgoing = call(
         prep_kernel,
         shape((owners, order // NB * my_rows + EXTRA, NB), BF16),
-        [SMEM, VMEM],
+        [HBM, HBM],
         VMEM,
+        [
+            pltpu.SMEM(table.shape, jnp.int32),
+            pltpu.VMEM((CHUNKS, my_rows, owners * order // CHUNKS), BF16),
+            DMA,
+            DMA((CHUNKS,)),
+        ],
         moved=4 * owners * my_rows * order,
     )(table, grad[0])
     received = lax.all_to_all(outgoing, "fsdp", split_axis=0, concat_axis=0, tiled=True)
@@ -289,23 +323,24 @@
     mine = call(sum_kernel, shape((groups, 1, NB), F32), [VMEM], VMEM, moved=64 * owners * NB)(received)
     sums = lax.all_to_all(mine, "grp", split_axis=0, concat_axis=0, tiled=True)
 
+    wide = pltpu.VMEM((2, order, order), F32)
     block, gram_part = call(
         gram_kernel,
         (shape((order, order), BF16), shape((2, order, order), F32)),
-        [VMEM, VMEM],
-        (VMEM, VMEM),
+        [VMEM, HBM],
+        (VMEM, HBM),
+        [pltpu.VMEM((2, order, order), BF16), wide, DMA((2,)), DMA((2,))],
         flops=8 * cube,
         moved=14 * order * order,
     )(received, basis_t)
 
-    wide = pltpu.VMEM((2, order, order), F32)
     small = pltpu.VMEM((2, NB, NB), F32)
     update, row_next, col_next = call(
         functools.partial(main_kernel, float(groups * owners * order * order)),
         (shape((order, order), BF16), shape((1, order), F32), shape((1, order), F32)),
-        [VMEM] * 6,
+        [VMEM, VMEM, VMEM, HBM, VMEM, VMEM],
         (VMEM, VMEM, VMEM),
-        [wide, wide, small, small, pltpu.VMEM((4, NB, NB), F32), pltpu.VMEM((2, NB, order), F32), pltpu.VMEM((2, order, order), BF16)],
+        [wide, DMA((2,)), wide, wide, small, small, pltpu.VMEM((4, NB, NB), F32), pltpu.VMEM((2, NB, order), F32), pltpu.VMEM((2, order, order), BF16)],
         flops=40 * cube,
         moved=20 * order * order,
         limit=24,

time: 120 us -> 121 us (level)
  no operation moved by 1% of the time
where the time goes in v3:
time: 121 us; the launch traced here: 120 us
  Pallas kernels  36.2 us (30%)
  starting transfers between devices  30.6 us (25%)
  waiting for transfers between devices  23.3 us (19%)
  blocking collectives  21.5 us (18%)
  local copies, waits for them, and re-layouts  8.12 us (7%)
    pallas_call x1, Pallas kernels, shards(): call(functools.partial(main_kernel, float(groups * owners * order * order...  28.9 us
    all_to_all x1, blocking collectives, shards(): lax.all_to_all(pieces, 'fsdp', split_axis=0, concat_axis=0, tiled=True)  21.5 us
    all_to_all x1, starting transfers between devices, shards(): lax.all_to_all(outgoing, 'fsdp', split_axis=0, concat_axis=0, tiled=True)  17.5 us
    all_to_all x1, waiting for transfers between devices, shards(): lax.all_to_all(outgoing, 'fsdp', split_axis=0, concat_axis=0, tiled=True)  15.5 us
    all_to_all x1, starting transfers between devices, shards(): sums = lax.all_to_all(mine, 'grp', split_axis=0, concat_axis=0, tiled=True)  13.1 us
    unnamed x30, local copies, waits for them, and re-layouts  8.12 us
    all_to_all x1, waiting for transfers between devices, shards(): sums = lax.all_to_all(mine, 'grp', split_axis=0, concat_axis=0, tiled=True)  7.78 us
    pallas_call x1, Pallas kernels, shards(): call(gram_kernel, (shape((order, order), BF16), shape((2, order, order),...  2.92 us
  transfers between devices with their start and end apart: 2, of which 2 were waited for; matrix products, arithmetic and copies ran while one was open for 0% of the time, Pallas kernels for 3%

profile of v3, /device:TPU:1, one launch (start us, length us, event | category | flops | bytes accessed | tf_op | source)
XLA Modules:
  0.0 120.5 jit_solution(2181883007823678312)
XLA Ops:
  0.6 0.0 copy-start
  0.6 1.0 copy-done
  1.7 0.0 copy-start.5
  1.7 0.7 copy-done.5
  2.3 1.6 %shard_map.103 = bf16[16,144,128]{2,1,0:T(8,128)(2,1)} custom-call(s32[1,16]{1,0:T(1,128)S(1)} %copy-done.5, bf16[32,8192]{1,0:T(8,128)(2,1)S(1)} %bitcast.11), custom_call_target="tpu_custom_call" | custom-call | bytes 1048576 | tf_op jit(solution)/shard_map/pallas_call | solution.py:299
  4.0 17.5 %all-to-all-start = ((bf16[16,144,128]{2,1,0:T(8,128)(2,1)}), bf16[16,144,128]{2,1,0:T(8,128)(2,1)S(1)}, u32[]{:S(2)}, u32[]{:S(2)}) async-start(bf16[16,144,128]{2,1,0:T(8,128)(2,1)} %shard_map.103), calls=%async_computation | async-start | bytes 1179648 | tf_op jit(solution)/shard_map/all_to_all | solution.py:312
  21.5 0.0 copy-done.1
  21.5 0.0 copy-done.2
  21.5 0.0 copy-done.3
  21.6 0.0 copy-done.4
  21.6 0.7 shard_map.105
  22.3 0.0 copy-start.7
  22.3 1.3 %copy-done.7 = f32[2,512,512]{2,1,0:T(8,128)} copy-done((f32[2,512,512]{2,1,0:T(8,128)}, f32[2,512,512]{2,1,0:T(8,128)S(1)}, u32[]{:S(2)}) %copy-start.7) | copy-done | bytes 2097176
  23.7 1.0 copy-done.9
  24.6 15.5 %all-to-all-done.block_ref.recv_ref = bf16[16,144,128]{2,1,0:T(8,128)(2,1)S(1)} async-done(((bf16[16,144,128]{2,1,0:T(8,128)(2,1)}), bf16[16,144,128]{2,1,0:T(8,128)(2,1)S(1)}, u32[]{:S(2)}, u32[]{:S(2)}) %all-to-all-start) | async-done | bytes 589856 | tf_op jit(solution)/shard_map/all_to_all | solution.py:312
  40.2 0.7 shard_map.104
  40.8 13.1 %all-to-all-start.1 = ((f32[64,1,128]{2,1,0:T(1,128)}), f32[64,1,128]{2,1,0:T(1,128)S(1)}, u32[]{:S(2)}, u32[]{:S(2)}) async-start(f32[64,1,128]{2,1,0:T(1,128)} %shard_map.104), calls=%async_computation.1 | async-start | bytes 65536 | tf_op jit(solution)/shard_map/all_to_all | solution.py:324
  53.9 0.0 copy-start.10
  53.9 1.2 %copy-done.10 = bf16[2,512,512]{2,1,0:T(8,128)(2,1)S(1)} copy-done((bf16[2,512,512]{2,1,0:T(8,128)(2,1)S(1)}, bf16[2,512,512]{2,1,0:T(8,128)(2,1)}, u32[]{:S(2)}) %copy-start.10) | copy-done | bytes 1048600
  55.1 2.9 %shard_map.106 = (bf16[512,512]{1,0:T(8,128)(2,1)S(1)}, f32[2,512,512]{2,1,0:T(8,128)S(1)}) custom-call(bf16[16,144,128]{2,1,0:T(8,128)(2,1)S(1)} %all-to-all-done.block_ref.recv_ref, bf16[2,512,512]{2,1,0:T(8,128)(2,1)S(1)} %copy-done.10), custom_call_target="tpu_custom_call" | custom-call | flops 2147483648 | bytes 3670016 | tf_op jit(solution)/shard_map/pallas_call | solution.py:327
  58.1 0.0 copy-start.13
  58.1 1.3 %copy-done.13 = f32[2,512,512]{2,1,0:T(8,128)} copy-done((f32[2,512,512]{2,1,0:T(8,128)}, f32[2,512,512]{2,1,0:T(8,128)S(1)}, u32[]{:S(2)}) %copy-start.13) | copy-done | bytes 2097176
  59.4 7.8 %all-to-all-done.1.sum_ref = f32[64,1,128]{2,1,0:T(1,128)S(1)} async-done(((f32[64,1,128]{2,1,0:T(1,128)}), f32[64,1,128]{2,1,0:T(1,128)S(1)}, u32[]{:S(2)}, u32[]{:S(2)}) %all-to-all-start.1) | async-done | bytes 32800 | tf_op jit(solution)/shard_map/all_to_all | solution.py:324
  67.1 0.0 copy-done.8
  67.1 0.0 copy-done.11
  67.1 0.0 copy-done.12
  67.1 0.0 copy-start.14
  67.2 1.6 %copy-done.14 = f32[2,512,512]{2,1,0:T(8,128)S(1)} copy-done((f32[2,512,512]{2,1,0:T(8,128)S(1)}, f32[2,512,512]{2,1,0:T(8,128)}, u32[]{:S(2)}) %copy-start.14) | copy-done | bytes 2097176
  68.7 28.9 %shard_map.107 = (bf16[512,512]{1,0:T(8,128)(2,1)S(1)}, f32[1,512]{1,0:T(1,128)}, f32[1,512]{1,0:T(1,128)}) custom-call(f32[64,1,128]{2,1,0:T(1,128)S(1)} %all-to-all-done.1.sum_ref, bf16[512,512]{1,0:T(8,128)(2,1)S(1)} %get-tuple-element.11.block_ref, f32[2,512,512]{2,1,0:T(8,128)S(1)} %copy-done.8, f32[2,512,512]{2,1,0:T(8,128)S(1)} %copy-done.14, ...), custom_call_target="tpu_custom_call" | custom-call | flops 10737418240 | bytes 5242880 | tf_op jit(solution)/shard_map/pallas_call | solution.py:338
  97.6 21.5 %all_to_all.15.back_ref = bf16[16,32,512]{2,1,0:T(8,128)(2,1)S(1)} all-to-all(bf16[16,32,512]{2,1,0:T(8,128)(2,1)S(1)} %bitcast.12), channel_id=1, replica_groups=mesh['fsdp'=16,'grp'=64] {'fsdp'}, dimensions={0} | all-to-all | bytes 1048576 | tf_op jit(solution)/shard_map/all_to_all | solution.py:350
  119.1 0.0 copy-done.6
  119.1 1.4 %shard_map.108 = bf16[32,8192]{1,0:T(8,128)(2,1)} custom-call(s32[1,16]{1,0:T(1,128)S(1)} %copy-done.6, bf16[16,32,512]{2,1,0:T(8,128)(2,1)S(1)} %all_to_all.15.back_ref), custom_call_target="tpu_custom_call" | custom-call | bytes 1048576 | tf_op jit(solution)/shard_map/pallas_call | solution.py:351
  (9 shorter events, 0.0 us)
Async XLA Ops:
  0.6 1.0 copy-start
  1.7 0.7 copy-start.5
  2.3 19.2 %copy-start.1 = (bf16[1,1,512,512]{3,2,1,0:T(8,128)(2,1)S(1)}, bf16[1,1,512,512]{3,2,1,0:T(8,128)(2,1)}, u32[]{:S(2)}) copy-start(bf16[1,1,512,512]{3,2,1,0:T(8,128)(2,1)} %param.10) | copy-start | bytes 1572868
  2.3 19.2 %copy-start.2 = (bf16[1,1,512,512]{3,2,1,0:T(8,128)(2,1)S(1)}, bf16[1,1,512,512]{3,2,1,0:T(8,128)(2,1)}, u32[]{:S(2)}) copy-start(bf16[1,1,512,512]{3,2,1,0:T(8,128)(2,1)} %param.11) | copy-start | bytes 1572868
  2.3 19.2 %copy-start.3 = (bf16[1,1,512,512]{3,2,1,0:T(8,128)(2,1)S(1)}, bf16[1,1,512,512]{3,2,1,0:T(8,128)(2,1)}, u32[]{:S(2)}) copy-start(bf16[1,1,512,512]{3,2,1,0:T(8,128)(2,1)} %param.12) | copy-start | bytes 1572868
  2.3 19.2 %copy-start.4 = (bf16[1,1,512,512]{3,2,1,0:T(8,128)(2,1)S(1)}, bf16[1,1,512,512]{3,2,1,0:T(8,128)(2,1)}, u32[]{:S(2)}) copy-start(bf16[1,1,512,512]{3,2,1,0:T(8,128)(2,1)} %param.13) | copy-start | bytes 1572868
  4.0 36.2 %all-to-all-start = ((bf16[16,144,128]{2,1,0:T(8,128)(2,1)}), bf16[16,144,128]{2,1,0:T(8,128)(2,1)S(1)}, u32[]{:S(2)}, u32[]{:S(2)}) async-start(bf16[16,144,128]{2,1,0:T(8,128)(2,1)} %shard_map.103), calls=%async_computation | async-start | bytes 1179648 | tf_op jit(solution)/shard_map/all_to_all | solution.py:312
  22.3 1.3 %copy-start.7 = (f32[2,512,512]{2,1,0:T(8,128)}, f32[2,512,512]{2,1,0:T(8,128)S(1)}, u32[]{:S(2)}) copy-start(f32[2,512,512]{2,1,0:T(8,128)S(1)} %get-tuple-element.12.stat_part) | copy-start | bytes 6291460
  23.7 1.0 copy-start.9
  40.8 26.3 %all-to-all-start.1 = ((f32[64,1,128]{2,1,0:T(1,128)}), f32[64,1,128]{2,1,0:T(1,128)S(1)}, u32[]{:S(2)}, u32[]{:S(2)}) async-start(f32[64,1,128]{2,1,0:T(1,128)} %shard_map.104), calls=%async_computation.1 | async-start | bytes 65536 | tf_op jit(solution)/shard_map/all_to_all | solution.py:324
  53.9 1.2 %copy-start.10 = (bf16[2,512,512]{2,1,0:T(8,128)(2,1)S(1)}, bf16[2,512,512]{2,1,0:T(8,128)(2,1)}, u32[]{:S(2)}) copy-start(bf16[2,512,512]{2,1,0:T(8,128)(2,1)} %copy-done.9) | copy-start | bytes 3145732
  55.1 12.0 %copy-start.8 = (f32[2,512,512]{2,1,0:T(8,128)S(1)}, f32[2,512,512]{2,1,0:T(8,128)}, u32[]{:S(2)}) copy-start(f32[2,512,512]{2,1,0:T(8,128)} %copy-done.7) | copy-start | bytes 6291460
  55.1 12.0 %copy-start.11 = (f32[1,1,512]{2,1,0:T(1,128)S(1)}, f32[1,1,512]{2,1,0:T(1,128)}, u32[]{:S(2)}) copy-start(f32[1,1,512]{2,1,0:T(1,128)} %param.14) | copy-start | bytes 6148
  55.1 12.0 %copy-start.12 = (f32[1,1,512]{2,1,0:T(1,128)S(1)}, f32[1,1,512]{2,1,0:T(1,128)}, u32[]{:S(2)}) copy-start(f32[1,1,512]{2,1,0:T(1,128)} %param.15) | copy-start | bytes 6148
  58.1 1.3 %copy-start.13 = (f32[2,512,512]{2,1,0:T(8,128)}, f32[2,512,512]{2,1,0:T(8,128)S(1)}, u32[]{:S(2)}) copy-start(f32[2,512,512]{2,1,0:T(8,128)S(1)} %get-tuple-element.13.gram_hbm) | copy-start | bytes 6291460
  67.1 1.6 %copy-start.14 = (f32[2,512,512]{2,1,0:T(8,128)S(1)}, f32[2,512,512]{2,1,0:T(8,128)}, u32[]{:S(2)}) copy-start(f32[2,512,512]{2,1,0:T(8,128)} %copy-done.13) | copy-start | bytes 6291460
  68.7 50.3 %copy-start.6 = (s32[1,16]{1,0:T(1,128)S(1)}, s32[1,16]{1,0:T(1,128)}, u32[]{:S(2)}) copy-start(s32[1,16]{1,0:T(1,128)} %table_ref.1) | copy-start | bytes 196

commit v4 on v2

--- a/solution.py
+++ b/solution.py
@@ -17,6 +17,7 @@
 NB = 128
 NT = NB // TILE
 EXTRA = 16
+CHUNKS = 4
 NN = (((1,), (0,)), ((), ()))
 NT_DIMS = (((1,), (1,)), ((), ()))
 TN = (((0,), (0,)), ((), ()))
@@ -108,13 +109,24 @@
             later = [s for s in later if next(s, later) is not later]
 
 
-def prep_kernel(table_ref, grad_ref, out_ref):
+def prep_kernel(table_hbm, grad_hbm, out_ref, table_ref, grad_ref, table_sem, grad_sem):
     owners, _, width = out_ref.shape
-    my_rows = grad_ref.shape[0]
-    order = grad_ref.shape[1] // owners
+    chunks, my_rows, span = grad_ref.shape
+    order = chunks * span // owners
+    table_copy = pltpu.make_async_copy(table_hbm, table_ref, table_sem)
+    table_copy.start()
+    copies = []
+    for g in range(chunks):
+        part = grad_hbm.at[:, g * span : (g + 1) * span]
+        copies.append(pltpu.make_async_copy(part, grad_ref.at[g], grad_sem.at[g]))
+        copies[g].start()
+    table_copy.wait()
     total = jnp.zeros((my_rows, order), F32)
     for j in range(owners):
-        part = grad_ref[:, j * order : (j + 1) * order]
+        g, first = divmod(j * order, span)
+        if first == 0:
+            copies[g].wait()
+        part = grad_ref[g, :, first : first + order]
         for c in range(order // width):
             out_ref[table_ref[0, j], c * my_rows : (c + 1) * my_rows, :] = part[:, c * width : (c + 1) * width]
         wide = part.astype(F32)
@@ -246,6 +258,8 @@
 
 VMEM = pl.BlockSpec(memory_space=pltpu.VMEM)
 SMEM = pl.BlockSpec(memory_space=pltpu.SMEM)
+HBM = pl.BlockSpec(memory_space=pltpu.HBM)
+DMA = pltpu.SemaphoreType.DMA
 
 
 def call(kernel, out_shapes, in_specs, out_specs, scratch=(), flops=0, moved=0, limit=12):
@@ -271,9 +285,16 @@
     outgoing = call(
         prep_kernel,
         shape((owners, order // NB * my_rows + EXTRA, NB), BF16),
-        [SMEM, VMEM],
+        [HBM, HBM],
         VMEM,
+        [
+            pltpu.SMEM(table.shape, jnp.int32),
+            pltpu.VMEM((CHUNKS, my_rows, owners * order // CHUNKS), BF16),
+            DMA,
+            DMA((CHUNKS,)),
+        ],
         moved=4 * owners * my_rows * order,
+        limit=63,
     )(table, grad[0])
     received = lax.all_to_all(outgoing, "fsdp", split_axis=0, concat_axis=0, tiled=True)
 

time: 120 us -> 119 us (level)
  waiting for transfers between devices: 23.9 us -> 20.8 us
  local copies, waits for them, and re-layouts: 8.12 us -> 9.55 us
    all_to_all x1, waiting for transfers between devices: 15.5 us -> 12.4 us  [shards(): lax.all_to_all(outgoing, 'fsdp', split_axis=0, concat_axis=0, tiled=True)]
    unnamed x30 -> x26, local copies, waits for them, and re-layouts: 8.12 us -> 9.55 us
where the time goes in v4:
time: 119 us
  Pallas kernels  35.9 us (30%)
  starting transfers between devices  30.6 us (26%)
  blocking collectives  21.5 us (18%)
  waiting for transfers between devices  20.8 us (17%)
  local copies, waits for them, and re-layouts  9.55 us (8%)
    pallas_call x1, Pallas kernels, shards(): call(functools.partial(main_kernel, float(groups * owners * order * order...  28.5 us
    all_to_all x1, blocking collectives, shards(): lax.all_to_all(pieces, 'fsdp', split_axis=0, concat_axis=0, tiled=True)  21.5 us
    all_to_all x1, starting transfers between devices, shards(): lax.all_to_all(outgoing, 'fsdp', split_axis=0, concat_axis=0, tiled=True)  17.5 us
    all_to_all x1, starting transfers between devices, shards(): sums = lax.all_to_all(mine, 'grp', split_axis=0, concat_axis=0, tiled=True)  13.1 us
    all_to_all x1, waiting for transfers between devices, shards(): lax.all_to_all(outgoing, 'fsdp', split_axis=0, concat_axis=0, tiled=True)  12.4 us
    unnamed x26, local copies, waits for them, and re-layouts  9.55 us
    all_to_all x1, waiting for transfers between devices, shards(): sums = lax.all_to_all(mine, 'grp', split_axis=0, concat_axis=0, tiled=True)  8.3 us
    pallas_call x1, Pallas kernels, shards(): call(gram_kernel, (shape((order, order), BF16), shape((2, order, order),...  2.38 us
  transfers between devices with their start and end apart: 2, of which 2 were waited for; matrix products, arithmetic and copies ran while one was open for 0% of the time, Pallas kernels for 3%

profile of v4, /device:TPU:1, one launch (start us, length us, event | category | flops | bytes accessed | tf_op | source)
XLA Modules:
  0.0 119.0 jit_solution(13911407494856239952)
XLA Ops:
  0.6 0.0 copy-start
  0.6 2.2 %shard_map.103 = bf16[16,144,128]{2,1,0:T(8,128)(2,1)} custom-call(s32[1,16]{1,0:T(1,128)} %table_ref.1, bf16[32,8192]{1,0:T(8,128)(2,1)} %bitcast.18), custom_call_target="tpu_custom_call" | custom-call | bytes 1048576 | tf_op jit(solution)/shard_map/pallas_call | solution.py:285
  2.8 17.5 %all-to-all-start = ((bf16[16,144,128]{2,1,0:T(8,128)(2,1)}), bf16[16,144,128]{2,1,0:T(8,128)(2,1)S(1)}, u32[]{:S(2)}, u32[]{:S(2)}) async-start(bf16[16,144,128]{2,1,0:T(8,128)(2,1)} %shard_map.103), calls=%async_computation | async-start | bytes 1179648 | tf_op jit(solution)/shard_map/all_to_all | solution.py:299
  20.4 0.0 copy-done
  20.4 0.0 copy-start.1
  20.4 1.0 copy-done.1
  21.4 0.0 copy-start.2
  21.4 1.0 copy-done.2
  22.5 1.0 copy-done.3
  23.5 0.7 shard_map.105
  24.2 0.0 copy-start.5
  24.2 1.3 %copy-done.5 = f32[2,512,512]{2,1,0:T(8,128)} copy-done((f32[2,512,512]{2,1,0:T(8,128)}, f32[2,512,512]{2,1,0:T(8,128)S(1)}, u32[]{:S(2)}) %copy-start.5) | copy-done | bytes 2097176
  25.6 0.0 copy-start.7
  25.6 1.0 copy-done.7
  26.6 12.4 %all-to-all-done.block_ref.recv_ref = bf16[16,144,128]{2,1,0:T(8,128)(2,1)S(1)} async-done(((bf16[16,144,128]{2,1,0:T(8,128)(2,1)}), bf16[16,144,128]{2,1,0:T(8,128)(2,1)S(1)}, u32[]{:S(2)}, u32[]{:S(2)}) %all-to-all-start) | async-done | bytes 589856 | tf_op jit(solution)/shard_map/all_to_all | solution.py:299
  39.0 0.7 shard_map.104
  39.7 13.1 %all-to-all-start.1 = ((f32[64,1,128]{2,1,0:T(1,128)}), f32[64,1,128]{2,1,0:T(1,128)S(1)}, u32[]{:S(2)}, u32[]{:S(2)}) async-start(f32[64,1,128]{2,1,0:T(1,128)} %shard_map.104), calls=%async_computation.1 | async-start | bytes 65536 | tf_op jit(solution)/shard_map/all_to_all | solution.py:311
  52.7 0.0 copy-start.8
  52.7 1.2 %copy-done.8 = bf16[2,512,512]{2,1,0:T(8,128)(2,1)S(1)} copy-done((bf16[2,512,512]{2,1,0:T(8,128)(2,1)S(1)}, bf16[2,512,512]{2,1,0:T(8,128)(2,1)}, u32[]{:S(2)}) %copy-start.8) | copy-done | bytes 1048600
  54.0 2.4 %shard_map.106 = (bf16[512,512]{1,0:T(8,128)(2,1)S(1)}, f32[2,512,512]{2,1,0:T(8,128)S(1)}) custom-call(bf16[16,144,128]{2,1,0:T(8,128)(2,1)S(1)} %all-to-all-done.block_ref.recv_ref, bf16[2,512,512]{2,1,0:T(8,128)(2,1)S(1)} %copy-done.8), custom_call_target="tpu_custom_call" | custom-call | flops 2147483648 | bytes 3670016 | tf_op jit(solution)/shard_map/pallas_call | solution.py:313
  56.3 0.0 copy-start.11
  56.4 1.3 %copy-done.11 = f32[2,512,512]{2,1,0:T(8,128)} copy-done((f32[2,512,512]{2,1,0:T(8,128)}, f32[2,512,512]{2,1,0:T(8,128)S(1)}, u32[]{:S(2)}) %copy-start.11) | copy-done | bytes 2097176
  57.7 8.3 %all-to-all-done.1.sum_ref = f32[64,1,128]{2,1,0:T(1,128)S(1)} async-done(((f32[64,1,128]{2,1,0:T(1,128)}), f32[64,1,128]{2,1,0:T(1,128)S(1)}, u32[]{:S(2)}, u32[]{:S(2)}) %all-to-all-start.1) | async-done | bytes 32800 | tf_op jit(solution)/shard_map/all_to_all | solution.py:311
  66.0 0.0 copy-done.6
  66.0 0.0 copy-done.9
  66.0 0.0 copy-done.10
  66.0 0.0 copy-start.12
  66.0 1.6 %copy-done.12 = f32[2,512,512]{2,1,0:T(8,128)S(1)} copy-done((f32[2,512,512]{2,1,0:T(8,128)S(1)}, f32[2,512,512]{2,1,0:T(8,128)}, u32[]{:S(2)}) %copy-start.12) | copy-done | bytes 2097176
  67.6 28.5 %shard_map.107 = (bf16[512,512]{1,0:T(8,128)(2,1)S(1)}, f32[1,512]{1,0:T(1,128)}, f32[1,512]{1,0:T(1,128)}) custom-call(f32[64,1,128]{2,1,0:T(1,128)S(1)} %all-to-all-done.1.sum_ref, bf16[512,512]{1,0:T(8,128)(2,1)S(1)} %get-tuple-element.11.block_ref, f32[2,512,512]{2,1,0:T(8,128)S(1)} %copy-done.6, f32[2,512,512]{2,1,0:T(8,128)S(1)} %copy-done.12, ...), custom_call_target="tpu_custom_call" | custom-call | flops 10737418240 | bytes 5242880 | tf_op jit(solution)/shard_map/pallas_call | solution.py:324
  96.1 21.5 %all_to_all.15.back_ref = bf16[16,32,512]{2,1,0:T(8,128)(2,1)S(1)} all-to-all(bf16[16,32,512]{2,1,0:T(8,128)(2,1)S(1)} %bitcast.11), channel_id=1, replica_groups=mesh['fsdp'=16,'grp'=64] {'fsdp'}, dimensions={0} | all-to-all | bytes 1048576 | tf_op jit(solution)/shard_map/all_to_all | solution.py:336
  117.6 0.0 copy-done.4
  117.6 1.4 %shard_map.108 = bf16[32,8192]{1,0:T(8,128)(2,1)} custom-call(s32[1,16]{1,0:T(1,128)S(1)} %copy-done.4, bf16[16,32,512]{2,1,0:T(8,128)(2,1)S(1)} %all_to_all.15.back_ref), custom_call_target="tpu_custom_call" | custom-call | bytes 1048576 | tf_op jit(solution)/shard_map/pallas_call | solution.py:337
  (5 shorter events, 0.0 us)
Async XLA Ops:
  0.6 19.7 %copy-start = (bf16[1,1,512,512]{3,2,1,0:T(8,128)(2,1)S(1)}, bf16[1,1,512,512]{3,2,1,0:T(8,128)(2,1)}, u32[]{:S(2)}) copy-start(bf16[1,1,512,512]{3,2,1,0:T(8,128)(2,1)} %param.10) | copy-start | bytes 1572868
  2.8 36.2 %all-to-all-start = ((bf16[16,144,128]{2,1,0:T(8,128)(2,1)}), bf16[16,144,128]{2,1,0:T(8,128)(2,1)S(1)}, u32[]{:S(2)}, u32[]{:S(2)}) async-start(bf16[16,144,128]{2,1,0:T(8,128)(2,1)} %shard_map.103), calls=%async_computation | async-start | bytes 1179648 | tf_op jit(solution)/shard_map/all_to_all | solution.py:299
  20.4 1.0 copy-start.1
  21.4 1.0 copy-start.2
  22.5 1.0 copy-start.3
  24.2 1.3 %copy-start.5 = (f32[2,512,512]{2,1,0:T(8,128)}, f32[2,512,512]{2,1,0:T(8,128)S(1)}, u32[]{:S(2)}) copy-start(f32[2,512,512]{2,1,0:T(8,128)S(1)} %get-tuple-element.12.stat_part) | copy-start | bytes 6291460
  25.6 1.0 copy-start.7
  39.7 26.3 %all-to-all-start.1 = ((f32[64,1,128]{2,1,0:T(1,128)}), f32[64,1,128]{2,1,0:T(1,128)S(1)}, u32[]{:S(2)}, u32[]{:S(2)}) async-start(f32[64,1,128]{2,1,0:T(1,128)} %shard_map.104), calls=%async_computation.1 | async-start | bytes 65536 | tf_op jit(solution)/shard_map/all_to_all | solution.py:311
  52.7 1.2 %copy-start.8 = (bf16[2,512,512]{2,1,0:T(8,128)(2,1)S(1)}, bf16[2,512,512]{2,1,0:T(8,128)(2,1)}, u32[]{:S(2)}) copy-start(bf16[2,512,512]{2,1,0:T(8,128)(2,1)} %copy-done.7) | copy-start | bytes 3145732
  54.0 12.0 %copy-start.6 = (f32[2,512,512]{2,1,0:T(8,128)S(1)}, f32[2,512,512]{2,1,0:T(8,128)}, u32[]{:S(2)}) copy-start(f32[2,512,512]{2,1,0:T(8,128)} %copy-done.5) | copy-start | bytes 6291460
  54.0 12.0 %copy-start.9 = (f32[1,1,512]{2,1,0:T(1,128)S(1)}, f32[1,1,512]{2,1,0:T(1,128)}, u32[]{:S(2)}) copy-start(f32[1,1,512]{2,1,0:T(1,128)} %param.14) | copy-start | bytes 6148
  54.0 12.0 %copy-start.10 = (f32[1,1,512]{2,1,0:T(1,128)S(1)}, f32[1,1,512]{2,1,0:T(1,128)}, u32[]{:S(2)}) copy-start(f32[1,1,512]{2,1,0:T(1,128)} %param.15) | copy-start | bytes 6148
  56.3 1.3 %copy-start.11 = (f32[2,512,512]{2,1,0:T(8,128)}, f32[2,512,512]{2,1,0:T(8,128)S(1)}, u32[]{:S(2)}) copy-start(f32[2,512,512]{2,1,0:T(8,128)S(1)} %get-tuple-element.13.gram_part) | copy-start | bytes 6291460
  66.0 1.6 %copy-start.12 = (f32[2,512,512]{2,1,0:T(8,128)S(1)}, f32[2,512,512]{2,1,0:T(8,128)}, u32[]{:S(2)}) copy-start(f32[2,512,512]{2,1,0:T(8,128)} %copy-done.11) | copy-start | bytes 6291460
  67.6 50.0 %copy-start.4 = (s32[1,16]{1,0:T(1,128)S(1)}, s32[1,16]{1,0:T(1,128)}, u32[]{:S(2)}) copy-start(s32[1,16]{1,0:T(1,128)} %table_ref.1) | copy-start | bytes 196
